TPU v7x, 32 devices: a whole 2x2x4 slice. The times are simulated.
32 devices in a mesh: gx: 16 (over z, y, x), gy: 2 (over core).
Axes of the slice: x: 2, y: 2, z: 4, core: 2. Of those that a mesh axis runs over, the one named last changes fastest.
Arguments:
- skip_feature_rows: bfloat16 [64, 192, 512], P(('gx', 'gy')), may hold values from -6 to 6
- coarse_features: bfloat16 [64, 192, 512], P(('gx', 'gy')), may hold values from -6 to 6
- cotangent: bfloat16 [64, 192, 512], P(('gx', 'gy')), may hold values from -6 to 6
- fine_coords: int32 [64, 3], P(('gx', 'gy')), may hold values from 0 to 3, as said below
- coarse_coords: int32 [64, 3], P(('gx', 'gy')), may hold values from 0 to 1, as said below
- parents: int32 [64], P(('gx', 'gy')), may hold values from 0 to 1
- counts: int32 [32], P(('gx', 'gy')), may hold values from 1 to 2
- conv_weight: bfloat16 [192, 27, 192], replicated, may hold values from -0.078125 to 0.078125
- up_weight: bfloat16 [8, 192, 192], replicated, may hold values from -0.4375 to 0.4375
Outputs:
- grad_skip: bfloat16 [64, 192, 512], P(('gx', 'gy'))
- grad_coarse: bfloat16 [64, 192, 512], P(('gx', 'gy'))
- grad_conv: float32 [192, 27, 192], P('gy')
Inputs may be any that keep to these rules, and one draw needn't show every extreme that they name: `fine_coords`: within one tile the fine slots have distinct coordinates in 0..1, 0..1, 0..3, and each equals 2 coarse_coords of its parent plus a 0/1 offset per axis. `coarse_coords`: within one tile the 2 coarse slots hold each coarse block position of the tile once.
All inputs are finite; a program needn't handle non-finite values.
Results may differ from a plain program's by a relative error of at most 0.013.
Values may be sent and summed in bfloat16 or wider, within the bound.
A program may use at most 128 MiB of HBM per device.

v0:
```python
import jax
import jax.numpy as jnp
from jax import lax
from jax.sharding import PartitionSpec as P

FB_X = 2
FB_Y = 2
FB_Z = 4


def padded_2(block, sides, width):
    for axis, dim in sides:
        count = lax.axis_size(axis)
        forward = [(i, i + 1) for i in range(count - 1)]
        backward = [(target, source) for source, target in forward]
        low = lax.ppermute(
            lax.slice_in_dim(block, block.shape[dim] - width, None, axis=dim), axis, forward
        )
        high = lax.ppermute(lax.slice_in_dim(block, 0, width, axis=dim), axis, backward)
        block = jnp.concatenate([low, block, high], axis=dim)
    return block


def index_tuple(anchor):
    return tuple((jnp.asarray(entry).astype(jnp.int32) for entry in anchor))


def add_into(target, addend, anchor):
    anchor = index_tuple(anchor)
    current = lax.dynamic_slice(target, anchor, addend.shape)
    return lax.dynamic_update_slice(target, current + addend, anchor)


def upsample(coarse_row, octant, up_rows):
    channel_count = coarse_row.shape[0]
    block_cube = coarse_row.reshape(channel_count, 8, 8, 8)
    octant_cube = lax.dynamic_slice(
        block_cube,
        index_tuple((0, 4 * octant[0], 4 * octant[1], 4 * octant[2])),
        (channel_count, 4, 4, 4),
    )
    product = jnp.dot(
        up_rows, octant_cube.reshape(channel_count, 64), preferred_element_type=jnp.float32
    )
    product = product.reshape(2, 2, 2, channel_count, 4, 4, 4).transpose(3, 4, 0, 5, 1, 6, 2)
    return product.reshape(channel_count, 512)


def fold_down(grad_row, up_rows):
    channel_count = grad_row.shape[0]
    regrouped = (
        grad_row.reshape(channel_count, 4, 2, 4, 2, 4, 2)
        .transpose(2, 4, 6, 0, 1, 3, 5)
        .reshape(8 * channel_count, 64)
    )
    return lax.dot_general(
        up_rows, regrouped, (((0,), (0,)), ((), ())), preferred_element_type=jnp.float32
    )


def coarse_gradient(grad_rows, parent_ids, octants, coarse_count, up_rows):
    channel_count = grad_rows.shape[1]
    coarse_total = jnp.zeros((coarse_count, channel_count, 8, 8, 8), jnp.float32)
    for member in range(grad_rows.shape[0]):
        addend = fold_down(grad_rows[member], up_rows).reshape(1, channel_count, 4, 4, 4)
        anchor = (
            parent_ids[member],
            0,
            4 * octants[member, 0],
            4 * octants[member, 1],
            4 * octants[member, 2],
        )
        coarse_total = add_into(coarse_total, addend, anchor)
    return coarse_total.astype(jnp.bfloat16).reshape(coarse_count, channel_count, 512)


def columns(padded, coord, reverse):
    channel_count = padded.shape[0]
    window = lax.dynamic_slice(
        padded,
        index_tuple((0, 8 * coord[0], 8 * coord[1], 8 * coord[2])),
        (channel_count, 10, 10, 10),
    )
    shifted = []
    for step_x in range(3):
        for step_y in range(3):
            for step_z in range(3):
                if reverse:
                    first_x, first_y, first_z = (2 - step_x, 2 - step_y, 2 - step_z)
                else:
                    first_x, first_y, first_z = (step_x, step_y, step_z)
                view = window[
                    :, first_x : first_x + 8, first_y : first_y + 8, first_z : first_z + 8
                ]
                shifted.append(view.reshape(channel_count, 512))
    return jnp.concatenate(shifted, 0)


def forward_slot(hidden_cols, cot_row, occupied, weight_flat):
    pre = jnp.dot(weight_flat, hidden_cols, preferred_element_type=jnp.float32)
    sigma = jax.nn.sigmoid(pre)
    return (cot_row.astype(jnp.float32) * (sigma * (1.0 + pre * (1.0 - sigma))) * occupied).astype(
        jnp.bfloat16
    )


def dense_volume(features, coords):
    channel_count = features.shape[1]
    volume = jnp.zeros((channel_count, 8 * FB_X, 8 * FB_Y, 8 * FB_Z), jnp.bfloat16)
    for member in range(features.shape[0]):
        anchor = index_tuple(
            (0, 8 * coords[member, 0], 8 * coords[member, 1], 8 * coords[member, 2])
        )
        volume = lax.dynamic_update_slice(
            volume, features[member].reshape(channel_count, 8, 8, 8), anchor
        )
    return volume


def pad_depth(volume):
    return jnp.pad(volume, ((0, 0), (0, 0), (0, 0), (1, 1)))


def local(
    skip_feature_rows,
    coarse_features,
    cotangent,
    fine_coords,
    coarse_coords,
    parents,
    counts,
    conv_weight,
    up_weight,
):
    slot_count = skip_feature_rows.shape[0]
    channel_count = skip_feature_rows.shape[1]
    coarse_count = coarse_features.shape[0]
    occupied = (jnp.arange(slot_count, dtype=jnp.int32) < counts[0]).astype(jnp.float32)
    up_rows = up_weight.reshape(8 * channel_count, channel_count)
    octants = fine_coords - 2 * coarse_coords[parents]
    lifted = jnp.stack(
        [
            upsample(coarse_features[parents[member]], octants[member], up_rows)
            for member in range(slot_count)
        ],
        0,
    )
    hidden = ((lifted + skip_feature_rows.astype(jnp.float32)) * occupied[:, None, None]).astype(
        jnp.bfloat16
    )
    hidden_frame = pad_depth(padded_2(dense_volume(hidden, fine_coords), (("gx", 1), ("gy", 2)), 1))
    weight_flat = conv_weight.reshape(channel_count, 27 * channel_count)
    weight_flipped = jnp.transpose(conv_weight, (2, 1, 0)).reshape(
        channel_count, 27 * channel_count
    )
    grad_list = []
    local_grad = jnp.zeros((channel_count, 27 * channel_count), jnp.float32)
    for member in range(slot_count):
        cols_one = columns(hidden_frame, fine_coords[member], False)
        grad_one = forward_slot(cols_one, cotangent[member], occupied[member], weight_flat)
        local_grad = local_grad + lax.dot_general(
            grad_one, cols_one, (((1,), (1,)), ((), ())), preferred_element_type=jnp.float32
        )
        grad_list.append(grad_one)
    grad_pre = jnp.stack(grad_list, 0)
    grad_frame = pad_depth(padded_2(dense_volume(grad_pre, fine_coords), (("gx", 1), ("gy", 2)), 1))
    skip_list = []
    for member in range(slot_count):
        grad_cols = columns(grad_frame, fine_coords[member], True)
        backprop_one = jnp.dot(weight_flipped, grad_cols, preferred_element_type=jnp.float32)
        skip_list.append((backprop_one * occupied[member]).astype(jnp.bfloat16))
    grad_skip = jnp.stack(skip_list, 0)
    grad_coarse = coarse_gradient(grad_skip, parents, octants, coarse_count, up_rows)
    row_share = lax.psum_scatter(
        local_grad.astype(jnp.bfloat16), "gy", scatter_dimension=0, tiled=True
    ).astype(jnp.float32)
    grad_conv = lax.psum(row_share, "gx")
    return (grad_skip, grad_coarse, grad_conv.reshape(grad_conv.shape[0], 27, channel_count))


def solution(mesh):
    in_specs = (
        P(("gx", "gy"), None, None),
        P(("gx", "gy"), None, None),
        P(("gx", "gy"), None, None),
        P(("gx", "gy"), None),
        P(("gx", "gy"), None),
        P(("gx", "gy")),
        P(("gx", "gy")),
        P(),
        P(),
    )
    out_specs = (P(("gx", "gy"), None, None), P(("gx", "gy"), None, None), P("gy", None, None))
    return jax.shard_map(local, mesh=mesh, in_specs=in_specs, out_specs=out_specs, check_vma=False)
```

profile of v0, /device:TPU:0, one launch (start us, length us, event | category | flops | bytes accessed | tf_op | source)
XLA Modules:
  0.0 308.8 jit_solution(10316095431266311941)
XLA Ops:
  34.3 4.9 %collective-permute-start = (bf16[192,1,16,32]{0,3,2,1:T(8,128)(2,1)S(1)}, bf16[192,1,16,32]{0,3,2,1:T(8,128)(2,1)S(1)}, u32[]{:S(2)}, u32[]{:S(2)}) collective-permute-start(bf16[192,1,16,32]{0,3,2,1:T(8,128)(2,1)S(1)} %get-tuple-element.120), channel_id=1, source_target_pairs={{0,2},{2,4},{4,6},{6,8},{8,10},{10,12},{12,14},{14,16},{16,18},{18... | collective-permute-start | bytes 589832 | tf_op jit(solution)/shard_map/ppermute | solution.py:16
  40.4 9.9 %collective-permute-done = bf16[192,1,16,32]{0,3,2,1:T(8,128)(2,1)S(1)} collective-permute-done((bf16[192,1,16,32]{0,3,2,1:T(8,128)(2,1)S(1)}, bf16[192,1,16,32]{0,3,2,1:T(8,128)(2,1)S(1)}, u32[]{:S(2)}, u32[]{:S(2)}) %collective-permute-start) | collective-permute-done | bytes 196640 | tf_op jit(solution)/shard_map/ppermute | solution.py:16
  56.7 3.4 %copy.21 = bf16[192,27,192]{0,2,1:T(8,128)(2,1)} copy(bf16[192,27,192]{2,0,1:T(8,128)(2,1)S(1)} %copy-done.3) | data formatting | bytes 3981312 | tf_op args[7]
  60.8 7.4 %fusion.11 = bf16[192,18,18,34]{0,3,2,1:T(8,128)(2,1)S(1)} fusion(bf16[192,18,1,32]{0,3,2,1:T(8,128)(2,1)} %collective-permute-done.3, bf16[192,18,1,32]{0,3,2,1:T(8,128)(2,1)} %collective-permute-done.2, bf16[192,1,16,32]{0,3,2,1:T(8,128)(2,1)} %copy-done.9, bf16[192,16,16,32]{0,3,2,1:T(8,128)(2,1)} %copy-done.1, bf16[192,1,16,32]{0,3,2,1:T(8,128)(2,1)} %copy-done.8), kind=kLoop, calls=%fused_computation.17 | loop fusion | flops 38071296 | bytes 8211456 | tf_op jit(solution)/shard_map/concatenate | solution.py:20
  68.2 10.6 %constant_dynamic-slice_fusion.106 = (bf16[192,8,8,8]{0,3,2,1:T(8,128)(2,1)}, bf16[192,8,8,8]{0,3,2,1:T(8,128)(2,1)}, bf16[192,8,8,8]{0,3,2,1:T(8,128)(2,1)}, bf...) fusion(bf16[192,18,18,34]{0,3,2,1:T(8,128)(2,1)S(1)} %fusion.11, ...), kind=kLoop, calls=%fused_computation.168 | loop fusion | bytes 21233736 | tf_op jit(solution)/shard_map/slice | solution.py:92
  78.9 10.2 %concatenate.26 = bf16[5184,512]{0,1:T(8,128)(2,1)} concatenate(bf16[192,512]{0,1:T(8,128)(2,1)} %bitcast.343, bf16[192,512]{0,1:T(8,128)(2,1)} %bitcast.342, bf16[192,512]{0,1:T(8,128)(2,1)} %bitcast.341, bf16[192,512]{0,1:T(8,128)(2,1)} %bitcast.340, bf16[192,512]{0,1:T(8,128)(2,1)} %bitcast.339, bf16[192,512]{0,1:T(8,128)(2,1)} %bitcast.338, bf16[192,512]{0,1:T(8,128)(2,1)} %bitcast.337, ...), dimensions={0} | concatenate | bytes 10616832 | tf_op jit(solution)/shard_map/concatenate | solution.py:96
  89.1 5.4 %convolution_bitcast_fusion.3 = f32[192,512]{1,0:T(8,128)S(1)} fusion(bf16[5184,512]{0,1:T(8,128)(2,1)} %concatenate.26, bf16[192,5184]{0,1:T(8,128)(2,1)} %bitcast.228), kind=kOutput, calls=%fused_computation.27 | convolution fusion | flops 1019215872 | bytes 7692288 | tf_op jit(solution)/shard_map/dot_general | solution.py:100
  94.6 3.9 %fusion.25 = f32[192,5184]{1,0:T(8,128)} fusion(bf16[5184,512]{0,1:T(8,128)(2,1)S(1)} %copy-done.4, f32[192,512]{1,0:T(8,128)S(1)} %convolution_bitcast_fusion.3, f32[]{:T(128)} %bitcast.54, bf16[2,192,512]{2,1,0:T(8,128)(2,1)S(1)} %copy-done.13), kind=kOutput, calls=%fused_computation.44 | convolution fusion | flops 1020297216 | bytes 9945092 | tf_op jit(solution)/shard_map/dot_general | solution.py:161
  98.5 10.2 %concatenate.27 = bf16[5184,512]{0,1:T(8,128)(2,1)} concatenate(bf16[192,512]{0,1:T(8,128)(2,1)} %bitcast.317, bf16[192,512]{0,1:T(8,128)(2,1)} %bitcast.316, bf16[192,512]{0,1:T(8,128)(2,1)} %bitcast.315, bf16[192,512]{0,1:T(8,128)(2,1)} %bitcast.314, bf16[192,512]{0,1:T(8,128)(2,1)} %bitcast.313, bf16[192,512]{0,1:T(8,128)(2,1)} %bitcast.312, bf16[192,512]{0,1:T(8,128)(2,1)} %bitcast.311, ...), dimensions={0} | concatenate | bytes 10616832 | tf_op jit(solution)/shard_map/concatenate | solution.py:96
  108.7 8.9 %fusion.21 = (bf16[192,512]{1,0:T(8,128)(2,1)}, bf16[192,512]{1,0:T(8,128)(2,1)}, f32[192,512]{1,0:T(8,128)S(1)}) fusion(f32[]{:T(128)} %bitcast.85, bf16[2,192,512]{2,1,0:T(8,128)(2,1)} %param.11, f32[]{:T(128)} %bitcast.54, f32[192,512]{1,0:T(8,128)} %copy-done.10, bf16[5184,512]{0,1:T(8,128)(2,1)} %concatenate.27, bf16[192,5184]{0,1:T(8,128)(2,1)} %bitcast.229), kind=kOutput, calls=%fused_computation.40 | convolution fusion | flops 1021378560 | bytes 8871944 | tf_op jit(solution)/shard_map/dot_general | solution.py:100
  117.6 3.3 %fusion.1 = bf16[192,5184]{1,0:T(8,128)(2,1)} fusion(f32[192,5184]{1,0:T(8,128)S(1)} %copy-done.5, bf16[5184,512]{0,1:T(8,128)(2,1)S(1)} %copy-done.2, f32[192,512]{1,0:T(8,128)S(1)} %get-tuple-element.144, f32[]{:T(128)} %bitcast.85, bf16[2,192,512]{2,1,0:T(8,128)(2,1)S(1)} %copy-done.14), kind=kOutput, calls=%fused_computation.5 | convolution fusion | flops 1022287872 | bytes 11984900 | tf_op jit(solution)/shard_map/dot_general | solution.py:161
  127.3 3.4 %collective-permute-start.4 = (bf16[192,1,16,32]{0,3,2,1:T(8,128)(2,1)S(1)}, bf16[192,1,16,32]{0,3,2,1:T(8,128)(2,1)S(1)}, u32[]{:S(2)}, u32[]{:S(2)}) collective-permute-start(bf16[192,1,16,32]{0,3,2,1:T(8,128)(2,1)S(1)} %get-tuple-element.118), channel_id=1, source_target_pairs={{0,2},{2,4},{4,6},{6,8},{8,10},{10,12},{12,14},{14,16},{16,18},{18... | collective-permute-start | bytes 589832 | tf_op jit(solution)/shard_map/ppermute | solution.py:16
  132.0 4.8 %collective-permute-done.4 = bf16[192,1,16,32]{0,3,2,1:T(8,128)(2,1)S(1)} collective-permute-done((bf16[192,1,16,32]{0,3,2,1:T(8,128)(2,1)S(1)}, bf16[192,1,16,32]{0,3,2,1:T(8,128)(2,1)S(1)}, u32[]{:S(2)}, u32[]{:S(2)}) %collective-permute-start.4) | collective-permute-done | bytes 196640 | tf_op jit(solution)/shard_map/ppermute | solution.py:16
  136.8 5.8 %collective-permute-done.5 = bf16[192,1,16,32]{0,3,2,1:T(8,128)(2,1)S(1)} collective-permute-done((bf16[192,1,16,32]{0,3,2,1:T(8,128)(2,1)S(1)}, bf16[192,1,16,32]{0,3,2,1:T(8,128)(2,1)S(1)}, u32[]{:S(2)}, u32[]{:S(2)}) %collective-permute-start.5) | collective-permute-done | bytes 196640 | tf_op jit(solution)/shard_map/ppermute | solution.py:19
  142.7 2.6 collective-permute-start.6
  148.8 7.2 %select_maximum_fusion = bf16[192,18,18,34]{0,3,2,1:T(8,128)(2,1)} fusion(bf16[192,18,1,32]{0,3,2,1:T(8,128)(2,1)S(1)} %collective-permute-done.7, bf16[192,18,1,32]{0,3,2,1:T(8,128)(2,1)S(1)} %collective-permute-done.6, bf16[192,1,16,32]{0,3,2,1:T(8,128)(2,1)S(1)} %collective-permute-done.5, ...), kind=kLoop, calls=%fused_computation.6 | loop fusion | flops 38071296 | bytes 8211456 | tf_op jit(solution)/shard_map/concatenate | solution.py:20
  156.1 2.8 copy.28
  158.9 20.9 %constant_dynamic-slice_fusion.105 = (bf16[192,8,8,8]{0,3,2,1:T(8,128)(2,1)}, bf16[192,8,8,8]{0,3,2,1:T(8,128)(2,1)}, bf16[192,8,8,8]{0,3,2,1:T(8,128)(2,1)}, bf...) fusion(bf16[192,18,18,34]{0,3,2,1:T(8,128)(2,1)} %select_maximu, ...), kind=kLoop, calls=%fused_computation.166 | loop fusion | bytes 21233736 | tf_op jit(solution)/shard_map/slice | solution.py:92
  179.8 10.3 %concatenate.30 = bf16[5184,512]{0,1:T(8,128)(2,1)} concatenate(bf16[192,512]{0,1:T(8,128)(2,1)} %bitcast.290, bf16[192,512]{0,1:T(8,128)(2,1)} %bitcast.289, bf16[192,512]{0,1:T(8,128)(2,1)} %bitcast.288, bf16[192,512]{0,1:T(8,128)(2,1)} %bitcast.287, bf16[192,512]{0,1:T(8,128)(2,1)} %bitcast.286, bf16[192,512]{0,1:T(8,128)(2,1)} %bitcast.285, bf16[192,512]{0,1:T(8,128)(2,1)} %bitcast.284, ...), dimensions={0} | concatenate | bytes 10616832 | tf_op jit(solution)/shard_map/concatenate | solution.py:96
  190.1 5.7 %fusion.16 = bf16[512,192]{0,1:T(8,128)(2,1)} fusion(bf16[5184,512]{0,1:T(8,128)(2,1)} %concatenate.30, bf16[192,5184]{0,1:T(8,128)(2,1)S(1)} %bitcast.225, f32[]{:T(128)} %bitcast.54), kind=kOutput, calls=%fused_computation.28 | convolution fusion | flops 1019412480 | bytes 7495684 | tf_op jit(solution)/shard_map/dot_general | solution.py:170
  205.1 10.2 %concatenate.31 = bf16[5184,512]{0,1:T(8,128)(2,1)} concatenate(bf16[192,512]{0,1:T(8,128)(2,1)} %bitcast.262, bf16[192,512]{0,1:T(8,128)(2,1)} %bitcast.261, bf16[192,512]{0,1:T(8,128)(2,1)} %bitcast.260, bf16[192,512]{0,1:T(8,128)(2,1)} %bitcast.259, bf16[192,512]{0,1:T(8,128)(2,1)} %bitcast.258, bf16[192,512]{0,1:T(8,128)(2,1)} %bitcast.257, bf16[192,512]{0,1:T(8,128)(2,1)} %bitcast.256, ...), dimensions={0} | concatenate | bytes 10616832 | tf_op jit(solution)/shard_map/concatenate | solution.py:96
  215.3 5.8 %fusion.17 = bf16[512,192]{0,1:T(8,128)(2,1)} fusion(bf16[5184,512]{0,1:T(8,128)(2,1)} %concatenate.31, bf16[192,5184]{0,1:T(8,128)(2,1)S(1)} %bitcast.226, f32[]{:T(128)} %bitcast.85), kind=kOutput, calls=%fused_computation.29 | convolution fusion | flops 1019412480 | bytes 7495684 | tf_op jit(solution)/shard_map/dot_general | solution.py:170
  225.2 73.3 %all-reduce.4.cloned.1.call-done = f32[96,27,192]{0,2,1:T(8,128)} async-done(((f32[96,27,192]{0,2,1:T(8,128)}), f32[96,27,192]{0,2,1:T(8,128)}) %all-reduce.4.cloned.1.call-update) | async-done | bytes 1990672 | tf_op jit(solution)/shard_map/psum | solution.py:177
  298.5 3.5 %copy.30 = f32[96,27,192]{2,0,1:T(8,128)} copy(f32[96,27,192]{0,2,1:T(8,128)} %all-reduce.4.cloned.1.call-done) | data formatting | bytes 3981312
  (102 shorter events, 47.5 us)
Async XLA Ops:
  7.2 19.0 %copy-start = (bf16[8,192,192]{2,1,0:T(8,128)(2,1)S(1)}, bf16[8,192,192]{2,1,0:T(8,128)(2,1)}, u32[]{:S(2)}) copy-start(bf16[8,192,192]{2,1,0:T(8,128)(2,1)} %param.17) | copy-start | bytes 1769476
  7.2 23.0 %copy-start.11 = (bf16[2,192,512]{2,1,0:T(8,128)(2,1)S(1)}, bf16[2,192,512]{2,1,0:T(8,128)(2,1)}, u32[]{:S(2)}) copy-start(bf16[2,192,512]{2,1,0:T(8,128)(2,1)} %param.9) | copy-start | bytes 1179652
  7.2 148.9 %reduce-scatter.2.cloned.1.call-start = ((), (), s32[]{:S(2)}) async-start(), calls=%async_computation.1 | async-start | bytes 3022848 | tf_op jit(solution)/shard_map/reduce_scatter | solution.py:174
  31.4 25.3 %copy-start.3 = (bf16[192,27,192]{2,0,1:T(8,128)(2,1)S(1)}, bf16[192,27,192]{2,0,1:T(8,128)(2,1)}, u32[]{:S(2)}) copy-start(bf16[192,27,192]{2,0,1:T(8,128)(2,1)} %param.16) | copy-start | bytes 5971972
  34.2 18.0 %copy-start.1 = (bf16[192,16,16,32]{0,3,2,1:T(8,128)(2,1)}, bf16[192,16,16,32]{0,3,2,1:T(8,128)(2,1)S(1)}, u32[]{:S(2)}) copy-start(bf16[192,16,16,32]{0,3,2,1:T(8,128)(2,1)S(1)} %constant_dynamic-update-slice_fusion.3) | copy-start | bytes 9437188
  34.3 16.1 %collective-permute-start = (bf16[192,1,16,32]{0,3,2,1:T(8,128)(2,1)S(1)}, bf16[192,1,16,32]{0,3,2,1:T(8,128)(2,1)S(1)}, u32[]{:S(2)}, u32[]{:S(2)}) collective-permute-start(bf16[192,1,16,32]{0,3,2,1:T(8,128)(2,1)S(1)} %get-tuple-element.120), channel_id=1, source_target_pairs={{0,2},{2,4},{4,6},{6,8},{8,10},{10,12},{12,14},{14,16},{16,18},{18... | collective-permute-start | bytes 589832 | tf_op jit(solution)/shard_map/ppermute | solution.py:16
  39.1 13.1 %collective-permute-start.1 = (bf16[192,1,16,32]{0,3,2,1:T(8,128)(2,1)S(1)}, bf16[192,1,16,32]{0,3,2,1:T(8,128)(2,1)S(1)}, u32[]{:S(2)}, u32[]{:S(2)}) collective-permute-start(bf16[192,1,16,32]{0,3,2,1:T(8,128)(2,1)S(1)} %get-tuple-element.121), channel_id=1, source_target_pairs={{2,0},{4,2},{6,4},{8,6},{10,8},{12,10},{14,12},{16,14},{18,16},{20... | collective-permute-start | bytes 589832 | tf_op jit(solution)/shard_map/ppermute | solution.py:19
  50.3 2.9 copy-start.8
  53.2 7.6 %collective-permute-start.2 = (bf16[192,18,1,32]{0,3,2,1:T(8,128)(2,1)}, bf16[192,18,1,32]{0,3,2,1:T(8,128)(2,1)}, u32[]{:S(2)}, u32[]{:S(2)}) collective-permute-start(bf16[192,18,1,32]{0,3,2,1:T(8,128)(2,1)} %get-tuple-element.116), channel_id=1, source_target_pairs={{0,1},{2,3},{4,5},{6,7},{8,9},{10,11},{12,13},{14,15},{16,17},{18,... | collective-permute-start | bytes 663560 | tf_op jit(solution)/shard_map/ppermute | solution.py:16
  55.2 5.6 %collective-permute-start.3 = (bf16[192,18,1,32]{0,3,2,1:T(8,128)(2,1)}, bf16[192,18,1,32]{0,3,2,1:T(8,128)(2,1)}, u32[]{:S(2)}, u32[]{:S(2)}) collective-permute-start(bf16[192,18,1,32]{0,3,2,1:T(8,128)(2,1)} %get-tuple-element.117), channel_id=1, source_target_pairs={{1,0},{3,2},{5,4},{7,6},{9,8},{11,10},{13,12},{15,14},{17,16},{19,... | collective-permute-start | bytes 663560 | tf_op jit(solution)/shard_map/ppermute | solution.py:19
  89.1 5.5 %copy-start.4 = (bf16[5184,512]{0,1:T(8,128)(2,1)S(1)}, bf16[5184,512]{0,1:T(8,128)(2,1)}, u32[]{:S(2)}) copy-start(bf16[5184,512]{0,1:T(8,128)(2,1)} %concatenate.26) | copy-start | bytes 15925252
  89.1 5.5 %copy-start.13 = (bf16[2,192,512]{2,1,0:T(8,128)(2,1)S(1)}, bf16[2,192,512]{2,1,0:T(8,128)(2,1)}, u32[]{:S(2)}) copy-start(bf16[2,192,512]{2,1,0:T(8,128)(2,1)} %param.11) | copy-start | bytes 1179652
  94.5 3.9 %copy-start.10 = (f32[192,512]{1,0:T(8,128)}, f32[192,512]{1,0:T(8,128)S(1)}, u32[]{:S(2)}) copy-start(f32[192,512]{1,0:T(8,128)S(1)} %convolution_bitcast_fusion.3) | copy-start | bytes 1179652
  108.7 8.9 %copy-start.2 = (bf16[5184,512]{0,1:T(8,128)(2,1)S(1)}, bf16[5184,512]{0,1:T(8,128)(2,1)}, u32[]{:S(2)}) copy-start(bf16[5184,512]{0,1:T(8,128)(2,1)} %concatenate.27) | copy-start | bytes 15925252
  108.7 8.9 %copy-start.5 = (f32[192,5184]{1,0:T(8,128)S(1)}, f32[192,5184]{1,0:T(8,128)}, u32[]{:S(2)}) copy-start(f32[192,5184]{1,0:T(8,128)} %fusion.25) | copy-start | bytes 11943940
  108.7 8.9 %copy-start.14 = (bf16[2,192,512]{2,1,0:T(8,128)(2,1)S(1)}, bf16[2,192,512]{2,1,0:T(8,128)(2,1)}, u32[]{:S(2)}) copy-start(bf16[2,192,512]{2,1,0:T(8,128)(2,1)} %param.11) | copy-start | bytes 1179652
  121.0 177.5 %all-reduce.4.cloned.1.call-start = ((), (), s32[]{:S(2)}) async-start(), calls=%async_computation.2 | async-start | bytes 5308416 | tf_op jit(solution)/shard_map/psum | solution.py:177
  127.3 9.5 %collective-permute-start.4 = (bf16[192,1,16,32]{0,3,2,1:T(8,128)(2,1)S(1)}, bf16[192,1,16,32]{0,3,2,1:T(8,128)(2,1)S(1)}, u32[]{:S(2)}, u32[]{:S(2)}) collective-permute-start(bf16[192,1,16,32]{0,3,2,1:T(8,128)(2,1)S(1)} %get-tuple-element.118), channel_id=1, source_target_pairs={{0,2},{2,4},{4,6},{6,8},{8,10},{10,12},{12,14},{14,16},{16,18},{18... | collective-permute-start | bytes 589832 | tf_op jit(solution)/shard_map/ppermute | solution.py:16
  130.7 11.9 %collective-permute-start.5 = (bf16[192,1,16,32]{0,3,2,1:T(8,128)(2,1)S(1)}, bf16[192,1,16,32]{0,3,2,1:T(8,128)(2,1)S(1)}, u32[]{:S(2)}, u32[]{:S(2)}) collective-permute-start(bf16[192,1,16,32]{0,3,2,1:T(8,128)(2,1)S(1)} %get-tuple-element.119), channel_id=1, source_target_pairs={{2,0},{4,2},{6,4},{8,6},{10,8},{12,10},{14,12},{16,14},{18,16},{20... | collective-permute-start | bytes 589832 | tf_op jit(solution)/shard_map/ppermute | solution.py:19
  142.7 3.9 %collective-permute-start.6 = (bf16[192,18,1,32]{0,3,2,1:T(8,128)(2,1)S(1)}, bf16[192,18,1,32]{0,3,2,1:T(8,128)(2,1)S(1)}, u32[]{:S(2)}, u32[]{:S(2)}) collective-permute-start(bf16[192,18,1,32]{0,3,2,1:T(8,128)(2,1)S(1)} %get-tuple-element.114), channel_id=1, source_target_pairs={{0,1},{2,3},{4,5},{6,7},{8,9},{10,11},{12,13},{14,15},{16,17},{18,... | collective-permute-start | bytes 663560 | tf_op jit(solution)/shard_map/ppermute | solution.py:16
  145.4 3.5 %collective-permute-start.7 = (bf16[192,18,1,32]{0,3,2,1:T(8,128)(2,1)S(1)}, bf16[192,18,1,32]{0,3,2,1:T(8,128)(2,1)S(1)}, u32[]{:S(2)}, u32[]{:S(2)}) collective-permute-start(bf16[192,18,1,32]{0,3,2,1:T(8,128)(2,1)S(1)} %get-tuple-element.115), channel_id=1, source_target_pairs={{1,0},{3,2},{5,4},{7,6},{9,8},{11,10},{13,12},{15,14},{17,16},{19,... | collective-permute-start | bytes 663560 | tf_op jit(solution)/shard_map/ppermute | solution.py:19
  215.3 8.0 %copy-start.12 = (f32[1,192,4,4,4]{1,4,3,2,0:T(4,128)S(1)}, f32[1,192,4,4,4]{1,4,3,2,0:T(4,128)}, u32[]{:S(2)}) copy-start(f32[1,192,4,4,4]{1,4,3,2,0:T(4,128)} %reshape.542) | copy-start | bytes 147460
  221.2 3.3 %copy-start.6 = (bf16[512,192]{0,1:T(8,128)(2,1)S(1)}, bf16[512,192]{0,1:T(8,128)(2,1)}, u32[]{:S(2)}) copy-start(bf16[512,192]{0,1:T(8,128)(2,1)} %fusion.16) | copy-start | bytes 589828
  221.2 3.3 %copy-start.7 = (bf16[512,192]{0,1:T(8,128)(2,1)S(1)}, bf16[512,192]{0,1:T(8,128)(2,1)}, u32[]{:S(2)}) copy-start(bf16[512,192]{0,1:T(8,128)(2,1)} %fusion.17) | copy-start | bytes 589828
  (1 other events, 0.9 us)
Sparse Core Ops, SparseCore 0:
  121.1 11.5 reduce-scatter.1
  159.0 139.3 all-reduce.3
where the time goes:
time: 314 us; the launch traced here: 309 us
  local copies, waits for them, and re-layouts  112 us (36%)
  waiting for transfers between devices  97.8 us (31%)
  matrix products  35.2 us (11%)
  between operations  26.8 us (9%)
  starting transfers between devices  18.5 us (6%)
  other arithmetic  18.3 us (6%)
    psum x1, waiting for transfers between devices, local(): grad_conv = lax.psum(row_share, 'gx')  73.3 us
    concatenate x4, local copies, waits for them, and re-layouts, columns(): return jnp.concatenate(shifted, 0)  41 us
    slice x2, local copies, waits for them, and re-layouts, columns(): window[:, first_x:first_x + 8, first_y:first_y + 8, first_z:first_z + 8]  31.5 us
    ppermute x4, waiting for transfers between devices, padded_2(): lax.ppermute(lax.slice_in_dim(block, block.shape[dim] - width, None, axis...  14.7 us
    concatenate x2, other arithmetic, padded_2(): block = jnp.concatenate([low, block, high], axis=dim)  14.7 us
    dot_general x2, matrix products, forward_slot(): pre = jnp.dot(weight_flat, hidden_cols, preferred_element_type=jnp.float32)  14.3 us
    ppermute x4, starting transfers between devices, padded_2(): lax.ppermute(lax.slice_in_dim(block, block.shape[dim] - width, None, axis...  12.9 us
    dot_general x2, matrix products, local(): jnp.dot(weight_flipped, grad_cols, preferred_element_type=jnp.float32)  11.6 us
  transfers between devices with their start and end apart: 10, of which 6 were waited for; matrix products, arithmetic and copies ran while one was open for 27% of the time, Pallas kernels for 0%

commit v1 on v0

v1 whole, which is shorter than its diff:
```python
import functools

import jax
import jax.numpy as jnp
from jax import lax
from jax.experimental import pallas as pl
from jax.experimental.pallas import tpu as pltpu
from jax.sharding import PartitionSpec as P

FB_X = 2
FB_Y = 2
MESH = pl.DeviceIdType.MESH
BF = jnp.bfloat16
F32 = jnp.float32
DIRS = ((-1, 0), (1, 0), (0, -1), (0, 1), (-1, -1), (-1, 1), (1, -1), (1, 1))
OPPOSITE = tuple(DIRS.index((-dx, -dy)) for dx, dy in DIRS)
NT = (((1,), (1,)), ((), ()))


def dot(a, b, dims=(((1,), (0,)), ((), ()))):
    return lax.dot_general(a, b, dims, preferred_element_type=F32)


def iota(shape, dim):
    return lax.broadcasted_iota(jnp.int32, shape, dim)


def one_hot(cond):
    return jnp.where(cond, 1.0, 0.0).astype(BF)


def identity(n):
    return one_hot(iota((n, n), 0) == iota((n, n), 1))


def child_row(v):
    p, q, s = v >> 6, (v >> 3) & 7, v & 7
    k = 4 * (p & 1) + 2 * (q & 1) + (s & 1)
    return k * 64 + (p >> 1) * 16 + (q >> 1) * 4 + (s >> 1)


def octant_column(u, meta, m):
    return (
        64 * (4 * meta[m, 3] + (u >> 4))
        + 8 * (4 * meta[m, 4] + ((u >> 2) & 3))
        + 4 * meta[m, 5]
        + (u & 3)
    )


def padded_rows(block, width):
    extra = width - block.shape[0]
    if extra == 0:
        return block
    return jnp.concatenate([block, jnp.zeros((extra, block.shape[1]), block.dtype)], 0)


class Exchange:
    def __init__(self, sizes, face_send, face_recv, edge_send, edge_recv, send_sem, recv_sem):
        gx, gy = lax.axis_index("gx"), lax.axis_index("gy")
        nx, ny = sizes
        self.refs = (face_send, face_recv, edge_send, edge_recv)
        self.sems = (send_sem, recv_sem)
        self.there, self.target = [], []
        for dx, dy in DIRS:
            x, y = gx + dx, gy + dy
            self.there.append((x >= 0) & (x < nx) & (y >= 0) & (y < ny))
            self.target.append((x, y))

    def greet(self):
        barrier = pltpu.get_barrier_semaphore()
        for d in range(8):
            @pl.when(self.there[d])
            def _():
                pl.semaphore_signal(barrier, inc=1, device_id=self.target[d], device_id_type=MESH)

    def await_greetings(self):
        peers = sum(there.astype(jnp.int32) for there in self.there)
        pl.semaphore_wait(pltpu.get_barrier_semaphore(), peers)

    def copy(self, d, landing):
        face_send, face_recv, edge_send, edge_recv = self.refs
        send, recv = (face_send, face_recv) if d < 4 else (edge_send, edge_recv)
        return pltpu.make_async_remote_copy(
            src_ref=send.at[d % 4],
            dst_ref=recv.at[landing % 4],
            send_sem=self.sems[0].at[d],
            recv_sem=self.sems[1].at[landing],
            device_id=self.target[d],
            device_id_type=MESH,
        )

    def pack(self, own, info):
        face_send, face_recv, edge_send, edge_recv = self.refs
        for d, (dx, dy) in enumerate(DIRS):
            x = 7 if dx > 0 else 0
            y = 7 if dy > 0 else 0
            if d < 2:
                face_send[d, 0:8] = own[8 * x : 8 * x + 8]
            elif d < 4:
                for i in range(8):
                    face_send[d, i] = own[8 * i + y]
            else:
                edge_send[d - 4, 0] = own[8 * x + y]
            if d < 4:
                face_send[d, 8:11] = info[...]
            else:
                edge_send[d - 4, 1:4] = info[...]

    def start(self):
        _, face_recv, _, edge_recv = self.refs
        for d in range(8):
            @pl.when(self.there[d])
            def _():
                self.copy(d, OPPOSITE[d]).start()

            @pl.when(jnp.logical_not(self.there[d]))
            def _():
                recv = face_recv if d < 4 else edge_recv
                recv[d % 4] = jnp.zeros(recv.shape[1:], recv.dtype)

    def finish(self):
        for d in range(8):
            @pl.when(self.there[d])
            def _():
                copy = self.copy(d, d)
                copy.wait_send()
                copy.wait_recv()


def weights_of(place, meta, m, dx, dy):
    x, y, z = place
    base = [meta[m, i].astype(F32) for i in range(3)]
    same = (x == base[0] + float(dx)) & (y == base[1] + float(dy))
    step = z - base[2]
    here = jnp.where(same & (step == 0.0), 1.0, 0.0)
    below = jnp.where(same & (step == -1.0), 1.0, 0.0)
    above = jnp.where(same & (step == 1.0), 1.0, 0.0)
    level = iota(here.shape, 0)
    return jnp.where(level == 0, below, here), here, jnp.where(level == 7, above, here)


def shifted(block):
    width = block.shape[-1]
    flat = block.reshape(-1, 8, width)
    down = pltpu.roll(flat, 1, 1).reshape(block.shape)
    up = pltpu.roll(flat, 7, 1).reshape(block.shape)
    return down, block, up


def sum_sources(sources):
    total = None
    for block, weights in sources:
        terms = [part * weight for part, weight in zip(shifted(block), weights)]
        total = terms if total is None else [a + b for a, b in zip(total, terms)]
    return total


def put(window, at_x, at_y, per_slot):
    width = per_slot[0][0].shape[-1]
    for k in range(3):
        both = jnp.concatenate([parts[k] for parts in per_slot], 1).astype(BF)
        rows = both.shape[0]
        if at_x is None:
            for i in range(rows):
                window[i + 1, at_y, :, k * width : (k + 1) * width] = both[i]
        elif at_y is None:
            window[at_x, 1 : 1 + rows, :, k * width : (k + 1) * width] = both
        else:
            window[at_x, at_y, :, k * width : (k + 1) * width] = both[0]


def own_place(meta, s, width):
    return [jnp.full((8, width), meta[s, i].astype(F32), F32) for i in range(3)]


def build_centre(window, own, meta, slots):
    width = own.shape[-1]
    ones = jnp.ones((8, width), F32)
    level = iota((8, width), 0)
    self_weights = (jnp.where(level == 0, 0.0, ones), ones, jnp.where(level == 7, 0.0, ones))
    other = [
        [(s, weights_of(own_place(meta, s, width), meta, m, 0, 0)) for s in range(slots) if s != m]
        for m in range(slots)
    ]

    def step(x, carry):
        rows = own[pl.ds(8 * x, 8)].astype(F32)
        blocks = [rows[:, 8 * s : 8 * s + 8] for s in range(slots)]
        per_slot = []
        for m in range(slots):
            sources = [(blocks[m], self_weights)] + [(blocks[s], w) for s, w in other[m]]
            per_slot.append(sum_sources(sources))
        put(window, x + 1, None, per_slot)
        return carry

    lax.fori_loop(0, 8, step, 0)


def build_border(window, own, face_recv, edge_recv, meta, slots):
    width = own.shape[-1]
    for dx, dy in DIRS:
        x = {-1: 7, 0: None, 1: 0}[dx]
        y = {-1: 7, 0: None, 1: 0}[dy]
        if dx and dy:
            own_rows = own[8 * x + y][None]
        elif dx:
            own_rows = own[8 * x : 8 * x + 8]
        else:
            own_rows = jnp.stack([own[8 * i + y] for i in range(8)], 0)
        own_rows = own_rows.astype(F32)
        tiles = []
        if dx:
            ref, d = face_recv, DIRS.index((dx, 0))
            rows = ref[d, y : y + 1] if dy else ref[d, 0:8]
            tiles.append((rows, ref[d, 8:11], dx, 0))
        if dy:
            ref, d = face_recv, DIRS.index((0, dy))
            rows = ref[d, x : x + 1] if dx else ref[d, 0:8]
            tiles.append((rows, ref[d, 8:11], 0, dy))
        if dx and dy:
            d = DIRS.index((dx, dy)) - 4
            tiles.append((edge_recv[d, 0:1], edge_recv[d, 1:4], dx, dy))
        tiles = [(rows.astype(F32), info.astype(F32), tx, ty) for rows, info, tx, ty in tiles]
        per_slot = []
        for m in range(slots):
            sources = []
            for s in range(slots):
                span = slice(8 * s, 8 * s + 8)
                if s != m:
                    place = own_place(meta, s, width)
                    sources.append((own_rows[:, span], weights_of(place, meta, m, dx, dy)))
                for rows, info, tx, ty in tiles:
                    place = (
                        info[0, span] + float(FB_X * tx),
                        info[1, span] + float(FB_Y * ty),
                        info[2, span],
                    )
                    sources.append((rows[:, span], weights_of(place, meta, m, dx, dy)))
            per_slot.append(sum_sources(sources))
        put(
            window,
            None if not dx else (0 if dx < 0 else 9),
            None if not dy else (0 if dy < 0 else 9),
            per_slot,
        )


def patch(window, j):
    x, y = j // 3, j % 3
    view = window[pl.ds(x, 8), pl.ds(y, 8)]
    return view.reshape(64 * view.shape[2], view.shape[3])


def forward_kernel(
    sizes, meta, info, skip, coarse, cot, up, weight, grad_pre, grad_weight,
    own, window, acc, turned, face_send, face_recv, edge_send, edge_recv, send_sem, recv_sem,
):
    slots, channels, voxels = skip.shape
    width = own.shape[-1]
    exchange = Exchange(sizes, face_send, face_recv, edge_send, edge_recv, send_sem, recv_sem)
    exchange.greet()
    eye = identity(voxels)
    spread = one_hot(
        iota((voxels, voxels), 1) == child_row(iota((voxels, voxels), 0))
    )
    rows = []
    for m in range(slots):
        octant = None
        column = octant_column(iota((64, voxels), 0), meta, m)
        for n in range(coarse.shape[0]):
            pick = one_hot((iota((64, voxels), 1) == column) & (meta[m, 6] == n))
            part = dot(pick, padded_rows(coarse[n], width), NT)
            octant = part if octant is None else octant + part
        lifted = dot(octant.astype(BF), up[...], NT)
        lifted = jnp.concatenate([lifted[:, k * width : (k + 1) * width] for k in range(8)], 0)
        high = lifted.astype(BF)
        low = (lifted - high.astype(F32)).astype(BF)
        total = dot(spread, high) + dot(spread, low) + dot(eye, padded_rows(skip[m], width), NT)
        rows.append((total * meta[m, 7].astype(F32)).reshape(64, 8, width))
    own[...] = jnp.concatenate(rows, 1).astype(BF)
    exchange.pack(own, info)
    exchange.await_greetings()
    exchange.start()
    build_centre(window, own, meta, slots)
    exchange.finish()
    build_border(window, own, face_recv, edge_recv, meta, slots)
    acc[...] = jnp.zeros_like(acc)

    def conv(j, carry):
        acc[...] += dot(patch(window, j), weight[j], NT)
        return carry

    lax.fori_loop(0, 9, conv, 0)
    pre_all = acc[...].reshape(64, 8 * slots, width)
    grads = []
    for m in range(slots):
        pre = pre_all[:, 8 * m : 8 * m + 8].reshape(voxels, width)
        sigma = 1.0 / (1.0 + jnp.exp(-pre))
        value = dot(eye, padded_rows(cot[m], width), NT)
        value = value * (sigma * (1.0 + pre * (1.0 - sigma))) * meta[m, 7].astype(F32)
        grads.append(value.reshape(64, 8, width))
    grad = jnp.concatenate(grads, 1)
    grad_pre[...] = grad.astype(BF)
    turned[...] = jnp.transpose(grad.reshape(64 * 8 * slots, width)).astype(BF)

    def outer(j, carry):
        grad_weight[j] = dot(turned[...], patch(window, j)).astype(BF)
        return carry

    lax.fori_loop(0, 9, outer, 0)


def backward_kernel(
    sizes, meta, info, own, up, weight, grad_skip, grad_coarse,
    window, acc, face_send, face_recv, edge_send, edge_recv, send_sem, recv_sem,
):
    slots, channels, voxels = grad_skip.shape
    width = own.shape[-1]
    exchange = Exchange(sizes, face_send, face_recv, edge_send, edge_recv, send_sem, recv_sem)
    exchange.greet()
    exchange.pack(own, info)
    exchange.await_greetings()
    exchange.start()
    build_centre(window, own, meta, slots)
    exchange.finish()
    build_border(window, own, face_recv, edge_recv, meta, slots)
    acc[...] = jnp.zeros_like(acc)

    def conv(j, carry):
        acc[...] += dot(patch(window, j), weight[j])
        return carry

    lax.fori_loop(0, 9, conv, 0)
    all_rows = acc[...].reshape(64, 8 * slots, width)
    gather = one_hot(iota((voxels, voxels), 0) == child_row(iota((voxels, voxels), 1)))
    folded = []
    for m in range(slots):
        rows = all_rows[:, 8 * m : 8 * m + 8].reshape(voxels, width) * meta[m, 7].astype(F32)
        grad_skip[m] = jnp.transpose(rows).astype(BF)[:channels]
        grouped = dot(gather, rows.astype(BF)).astype(BF)
        grouped = jnp.concatenate([grouped[64 * k : 64 * k + 64] for k in range(8)], 1)
        folded.append(jnp.transpose(dot(grouped, up[...])).astype(BF))
    for n in range(grad_coarse.shape[0]):
        total = None
        for m in range(slots):
            column = octant_column(iota((64, voxels), 0), meta, m)
            place = one_hot((iota((64, voxels), 1) == column) & (meta[m, 6] == n))
            part = dot(folded[m], place)
            total = part if total is None else total + part
        grad_coarse[n] = total.astype(BF)[:channels]


def exchange_scratch(slots, width):
    return [
        pltpu.VMEM((4, 11, 8 * slots, width), BF),
        pltpu.VMEM((4, 11, 8 * slots, width), BF),
        pltpu.VMEM((4, 4, 8 * slots, width), BF),
        pltpu.VMEM((4, 4, 8 * slots, width), BF),
        pltpu.SemaphoreType.DMA((8,)),
        pltpu.SemaphoreType.DMA((8,)),
    ]


def local(
    sizes, skip_feature_rows, coarse_features, cotangent, fine_coords, coarse_coords,
    parents, counts, conv_weight, up_weight,
):
    slots, channels, voxels = skip_feature_rows.shape
    width = -(-channels // 128) * 128
    extra = width - channels
    octants = fine_coords - 2 * coarse_coords[parents]
    occupied = (jnp.arange(slots, dtype=jnp.int32) < counts[0]).astype(jnp.int32)
    meta = jnp.concatenate([fine_coords, octants, parents[:, None], occupied[:, None]], 1)
    info = jnp.broadcast_to(
        jnp.repeat(fine_coords.T.astype(BF), 8, axis=1)[:, :, None], (3, 8 * slots, width)
    )
    up = jnp.pad(up_weight, ((0, 0), (0, extra), (0, extra))).reshape(8 * width, width)
    padded = jnp.pad(conv_weight, ((0, extra), (0, 0), (0, extra)))
    weight_forward = padded.reshape(width, 9, 3 * width).transpose(1, 0, 2)
    weight_backward = padded[:, ::-1].transpose(1, 0, 2).reshape(9, 3 * width, width)
    smem = pl.BlockSpec(memory_space=pltpu.SMEM)
    vmem = pl.BlockSpec(memory_space=pltpu.VMEM)
    window = pltpu.VMEM((10, 10, 8 * slots, 3 * width), BF)
    acc = pltpu.VMEM((64 * 8 * slots, width), F32)
    rows = jax.ShapeDtypeStruct((64, 8 * slots, width), BF)
    limit = 56 * 1024 * 1024
    flops = 2 * 27 * slots * voxels * channels * channels
    grad_pre, grad_weight = pl.pallas_call(
        functools.partial(forward_kernel, sizes),
        out_shape=(rows, jax.ShapeDtypeStruct((9, width, 3 * width), BF)),
        in_specs=[smem] + [vmem] * 6,
        out_specs=(vmem, vmem),
        scratch_shapes=[
            pltpu.VMEM(rows.shape, BF), window, acc,
            pltpu.VMEM((width, 64 * 8 * slots), BF),
        ] + exchange_scratch(slots, width),
        compiler_params=pltpu.CompilerParams(
            collective_id=0, has_side_effects=True, vmem_limit_bytes=limit
        ),
        cost_estimate=pl.CostEstimate(flops=2 * flops, bytes_accessed=12 << 20, transcendentals=0),
        name="forward",
    )(meta, info, skip_feature_rows, coarse_features, cotangent, up, weight_forward)
    grad_conv = grad_weight.reshape(9, width, 3, width)[:, :channels, :, :channels]
    grad_conv = grad_conv.transpose(1, 0, 2, 3).reshape(channels, 27 * channels)
    grad_conv = lax.psum_scatter(grad_conv, "gy", scatter_dimension=0, tiled=True)
    grad_conv = lax.psum(grad_conv, "gx").astype(F32)
    slab = jax.ShapeDtypeStruct((slots, channels, voxels), BF)
    coarse_slab = jax.ShapeDtypeStruct(coarse_features.shape, BF)
    grad_skip, grad_coarse = pl.pallas_call(
        functools.partial(backward_kernel, sizes),
        out_shape=(slab, coarse_slab),
        in_specs=[smem] + [vmem] * 4,
        out_specs=(vmem, vmem),
        scratch_shapes=[window, acc] + exchange_scratch(slots, width),
        compiler_params=pltpu.CompilerParams(
            collective_id=1, has_side_effects=True, vmem_limit_bytes=limit
        ),
        cost_estimate=pl.CostEstimate(flops=8 * flops, bytes_accessed=64 << 20, transcendentals=0),
        name="backward",
    )(meta, info, grad_pre, up, weight_backward)
    return (grad_skip, grad_coarse, grad_conv.reshape(grad_conv.shape[0], 27, channels))


def solution(mesh):
    in_specs = (
        P(("gx", "gy"), None, None),
        P(("gx", "gy"), None, None),
        P(("gx", "gy"), None, None),
        P(("gx", "gy"), None),
        P(("gx", "gy"), None),
        P(("gx", "gy")),
        P(("gx", "gy")),
        P(),
        P(),
    )
    out_specs = (P(("gx", "gy"), None, None), P(("gx", "gy"), None, None), P("gy", None, None))
    sizes = (mesh.shape["gx"], mesh.shape["gy"])
    return jax.shard_map(
        functools.partial(local, sizes),
        mesh=mesh,
        in_specs=in_specs,
        out_specs=out_specs,
        check_vma=False,
    )
```

time: 314 us -> 213 us (0.68); the launches traced: 309 us -> 212 us
  local copies, waits for them, and re-layouts: 112 us -> 42.5 us
  Pallas kernels: 0 us -> 46.4 us
  matrix products: 35.2 us -> 0 us
  starting transfers between devices: 18.5 us -> 0.08 us
  other arithmetic: 18.3 us -> 3.3 us
  between operations: 26.8 us -> 14.8 us
  waiting for transfers between devices: 97.8 us -> 105 us
    pallas_call x0 -> x2, Pallas kernels: none -> 46.4 us  [the longest x1 26.9 us: local(): pl.pallas_call(functools.partial(forward_kernel, sizes), out_shape=(rows,...]
    concatenate x4 -> x0, local copies, waits for them, and re-layouts: 41 us -> none  [columns(): return jnp.concatenate(shifted, 0)]
    dot_general x10 -> x0, matrix products: 35.2 us -> none  [the longest x2 14.3 us: forward_slot(): pre = jnp.dot(weight_flat, hidden_cols, preferred_element_type=jnp.float32)]
    slice x9 -> x1, local copies, waits for them, and re-layouts: 36.6 us -> 3.54 us  [local(): grad_weight.reshape(9, width, 3, width)[:, :channels, :, :channels]]
    psum x1, waiting for transfers between devices: 73.3 us -> 101 us  [local(): grad_conv = lax.psum(grad_conv, 'gx').astype(F32)]
    ppermute x8 -> x0, waiting for transfers between devices: 24.5 us -> none  [the longest x4 14.7 us: padded_2(): lax.ppermute(lax.slice_in_dim(block, block.shape[dim] - width, None, axis...]
    ppermute x8 -> x0, starting transfers between devices: 18.2 us -> none  [the longest x4 12.9 us: padded_2(): lax.ppermute(lax.slice_in_dim(block, block.shape[dim] - width, None, axis...]
    concatenate x2 -> x1, other arithmetic: 14.7 us -> 1.31 us  [local(): jnp.concatenate([fine_coords, octants, parents[:, None], occupied[:, None...]
  transfers between devices with their start and end apart: 10 -> 2, of which waited for: 6 -> 2; matrix products, arithmetic and copies ran while one was open for 27% -> 4% of each run, Pallas kernels for 0% -> 9%
where the time goes in v1:
time: 213 us; the launch traced here: 212 us
  waiting for transfers between devices  105 us (49%)
  Pallas kernels  46.4 us (22%)
  local copies, waits for them, and re-layouts  42.5 us (20%)
  between operations  14.8 us (7%)
  other arithmetic  3.3 us (2%)
    psum x1, waiting for transfers between devices, local(): grad_conv = lax.psum(grad_conv, 'gx').astype(F32)  101 us
    pallas_call x1, Pallas kernels, local(): pl.pallas_call(functools.partial(forward_kernel, sizes), out_shape=(rows,...  26.9 us
    pallas_call x1, Pallas kernels, local(): pl.pallas_call(functools.partial(backward_kernel, sizes), out_shape=(slab...  19.6 us
    unnamed x16, local copies, waits for them, and re-layouts  15.7 us
    transpose x2, local copies, waits for them, and re-layouts, local(): padded[:, ::-1].transpose(1, 0, 2).reshape(9, 3 * width, width)  7.76 us
    pallas_call x1, local copies, waits for them, and re-layouts, local(): pl.pallas_call(functools.partial(forward_kernel, sizes), out_shape=(rows,...  5.73 us
  transfers between devices with their start and end apart: 2, of which 2 were waited for; matrix products, arithmetic and copies ran while one was open for 4% of the time, Pallas kernels for 9%

profile of v1, /device:TPU:0, one launch (start us, length us, event | category | flops | bytes accessed | tf_op | source)
XLA Modules:
  0.0 212.2 jit_solution(1008453743669115631)
XLA Ops:
  7.9 0.7 compare_select_fusion
  8.6 0.6 compare_convert_fusion
  9.2 1.3 copy.21
  10.5 0.6 gather_fusion
  11.0 0.8 convert_bitcast_fusion
  12.1 4.5 %copy.23 = bf16[192,27,192]{0,2,1:T(8,128)(2,1)} copy(bf16[192,27,192]{2,0,1:T(8,128)(2,1)} %param.16) | data formatting | bytes 3981312 | tf_op args[7]
  16.6 1.1 pad.8
  17.7 2.3 %pad.9 = bf16[256,27,256]{0,2,1:T(8,128)(2,1)S(1)} pad(bf16[192,27,192]{0,2,1:T(8,128)(2,1)} %copy.23, bf16[]{:T(256)} %constant.2.clone.1), padding=0_64x0_0x0_64 | pad | bytes 5529602 | tf_op jit(solution)/shard_map/jit(_pad)/pad | solution.py:379
  20.0 3.6 %copy.24 = bf16[256,9,768]{2,0,1:T(8,128)(2,1)} copy(bf16[256,9,768]{0,2,1:T(8,128)(2,1)S(1)} %bitcast.17) | data formatting | bytes 7077888 | tf_op jit(solution)/shard_map/reshape | solution.py:380
  23.6 1.3 pad_add_fusion.meta
  24.9 0.7 broadcast_in_dim.21.info
  25.6 26.9 %forward.1 = (bf16[64,16,256]{2,1,0:T(8,128)(2,1)}, bf16[9,256,768]{2,1,0:T(8,128)(2,1)}) custom-call(s32[2,8]{1,0:T(2,128)} %pad_add_fusion.meta, bf16[3,16,256]{2,1,0:T(8,128)(2,1)} %broadcast_in_dim.21.info, bf16[2,192,512]{2,1,0:T(8,128)(2,1)} %skip.1, bf16[2,192,512]{2,1,0:T(8,128)(2,1)} %coarse.1, bf16[2,192,512]{2,1,0:T(8,128)(2,1)} %cot.1, ...), custom_call_target="tpu_custom_call" | custom-call | flops 4076863488 | bytes 12582912 | tf_op jit(solution)/shard_map/forward/pallas_call | solution.py:389
  52.5 5.7 %copy.26 = bf16[9,256,768]{1,2,0:T(8,128)(2,1)} copy(bf16[9,256,768]{2,1,0:T(8,128)(2,1)} %get-tuple-element.10) | data formatting | bytes 7077888 | tf_op jit(solution)/shard_map/forward/pallas_call | solution.py:389
  58.2 3.5 %slice.6 = bf16[9,192,3,192]{1,3,2,0:T(8,128)(2,1)} slice(bf16[9,256,3,256]{1,3,2,0:T(8,128)(2,1)} %bitcast.18), slice={[0:9], [0:192], [0:3], [0:192]} | slice | bytes 3981312 | tf_op jit(solution)/shard_map/slice | solution.py:404
  61.7 4.4 %copy.28 = bf16[192,5184]{1,0:T(8,128)(2,1)} copy(bf16[192,5184]{0,1:T(8,128)(2,1)} %bitcast.19) | data formatting | bytes 3981312
  66.2 2.0 reverse_bitcast_fusion
  68.2 5.7 %copy.25 = bf16[27,256,256]{2,1,0:T(8,128)(2,1)} copy(bf16[27,256,256]{1,2,0:T(8,128)(2,1)} %reverse_bitcast_fusion) | data formatting | bytes 7077888 | tf_op jit(solution)/shard_map/transpose | solution.py:381
  73.9 3.5 %reduce-scatter.4.cloned.1.call-done = bf16[96,5184]{1,0:T(8,128)(2,1)} async-done(((bf16[192,5184]{1,0:T(8,128)(2,1)}), bf16[96,5184]{1,0:T(8,128)(2,1)}) %reduce-scatter.4.cloned.1.call-update) | async-done | bytes 995344
  77.5 2.4 %copy.29 = bf16[96,5184]{0,1:T(8,128)(2,1)} copy(bf16[96,5184]{1,0:T(8,128)(2,1)} %reduce-scatter.4.cloned.1.call-done) | data formatting | bytes 1990656
  79.9 19.6 %backward.1 = (bf16[2,192,512]{2,1,0:T(8,128)(2,1)}, bf16[2,192,512]{2,1,0:T(8,128)(2,1)}) custom-call(s32[2,8]{1,0:T(2,128)} %pad_add_fusion.meta, bf16[3,16,256]{2,1,0:T(8,128)(2,1)} %broadcast_in_dim.21.info, bf16[64,16,256]{2,1,0:T(8,128)(2,1)} %get-tuple-element.7.own, bf16[2048,256]{1,0:T(8,128)(2,1)} %bitcast.24, bf16[9,768,256]{2,1,0:T(8,128)(2,1)} %bitcast.21), custom_call_target="tpu_custom_call" | custom-call | flops 16307453952 | bytes 67108864 | tf_op jit(solution)/shard_map/backward/pallas_call | solution.py:410
  99.5 101.4 %all-reduce.4.cloned.1.call-done = bf16[96,27,192]{0,2,1:T(8,128)(2,1)} async-done(((bf16[96,27,192]{0,2,1:T(8,128)(2,1)}), bf16[96,27,192]{0,2,1:T(8,128)(2,1)}) %all-reduce.4.cloned.1.call-update) | async-done | bytes 995344 | tf_op jit(solution)/shard_map/psum | solution.py:407
  200.9 2.9 %copy.27 = f32[96,27,192]{2,0,1:T(8,128)} copy(bf16[96,27,192]{0,2,1:T(8,128)(2,1)} %all-reduce.4.cloned.1.call-done) | data formatting | bytes 2985984
  203.8 0.7 copy.34
  204.6 0.7 copy.35
  (18 shorter events, 0.4 us)
Async XLA Ops:
  7.2 3.3 %copy-start = (s32[2,3]{1,0:T(2,128)S(1)}, s32[2,3]{1,0:T(2,128)}, u32[]{:S(2)}) copy-start(s32[2,3]{1,0:T(2,128)} %param.13) | copy-start | bytes 76
  7.2 9.4 %copy-start.1 = (bf16[8,192,192]{2,1,0:T(8,128)(2,1)S(1)}, bf16[8,192,192]{2,1,0:T(8,128)(2,1)}, u32[]{:S(2)}) copy-start(bf16[8,192,192]{2,1,0:T(8,128)(2,1)} %param.17) | copy-start | bytes 1769476
  7.2 70.3 %reduce-scatter.4.cloned.1.call-start = ((), (), s32[]{:S(2)}) async-start(), calls=%async_computation.2 | async-start | bytes 3022848
  20.0 3.6 %copy-start.4 = (s32[2,3]{1,0:T(2,128)S(1)}, s32[2,3]{1,0:T(2,128)}, u32[]{:S(2)}) copy-start(s32[2,3]{1,0:T(2,128)} %param.12) | copy-start | bytes 76
  66.1 134.8 %all-reduce.4.cloned.1.call-start = ((), (), s32[]{:S(2)}) async-start(), calls=%async_computation.1 | async-start | bytes 2654208 | tf_op jit(solution)/shard_map/psum | solution.py:407
  99.5 104.3 %copy-start.3 = (bf16[2,192,512]{2,1,0:T(8,128)(2,1)S(1)}, bf16[2,192,512]{2,1,0:T(8,128)(2,1)}, u32[]{:S(2)}) copy-start(bf16[2,192,512]{2,1,0:T(8,128)(2,1)} %get-tuple-element.22) | copy-start | bytes 1179652
  99.5 105.1 %copy-start.2 = (bf16[2,192,512]{2,1,0:T(8,128)(2,1)S(1)}, bf16[2,192,512]{2,1,0:T(8,128)(2,1)}, u32[]{:S(2)}) copy-start(bf16[2,192,512]{2,1,0:T(8,128)(2,1)} %get-tuple-element.23) | copy-start | bytes 1179652
Sparse Core Ops, SparseCore 0:
  66.2 11.1 reduce-scatter.3
  84.4 116.4 all-reduce.3

commit v2 on v1

--- a/solution.py
+++ b/solution.py
@@ -67,15 +67,18 @@
             self.there.append((x >= 0) & (x < nx) & (y >= 0) & (y < ny))
             self.target.append((x, y))
 
-    def greet(self):
+    def greet(self, others):
         barrier = pltpu.get_barrier_semaphore()
         for d in range(8):
             @pl.when(self.there[d])
             def _():
                 pl.semaphore_signal(barrier, inc=1, device_id=self.target[d], device_id_type=MESH)
 
-    def await_greetings(self):
-        peers = sum(there.astype(jnp.int32) for there in self.there)
+        for target in others:
+            pl.semaphore_signal(barrier, inc=1, device_id=target, device_id_type=MESH)
+
+    def await_greetings(self, others):
+        peers = len(others) + sum(there.astype(jnp.int32) for there in self.there)
         pl.semaphore_wait(pltpu.get_barrier_semaphore(), peers)
 
     def copy(self, d, landing):
@@ -103,9 +106,9 @@
             else:
                 edge_send[d - 4, 0] = own[8 * x + y]
             if d < 4:
-                face_send[d, 8:11] = info[...]
+                face_send[d, 8:11] = info
             else:
-                edge_send[d - 4, 1:4] = info[...]
+                edge_send[d - 4, 1:4] = info
 
     def start(self):
         _, face_recv, _, edge_recv = self.refs
@@ -252,18 +255,181 @@
     return view.reshape(64 * view.shape[2], view.shape[3])
 
 
-def forward_kernel(
-    sizes, meta, info, skip, coarse, cot, up, weight, grad_pre, grad_weight,
-    own, window, acc, turned, face_send, face_recv, edge_send, edge_recv, send_sem, recv_sem,
+class Ring:
+    def __init__(self, index, count, target, send_sem, recv_sem):
+        self.index, self.count = index, count
+        self.sems = (send_sem, recv_sem)
+        self.ranks = [lax.rem(index + r, count) for r in range(1, count)]
+        self.origins = [lax.rem(index + count - r, count) for r in range(1, count)]
+        self.targets = [target(rank) for rank in self.ranks]
+
+    def copies(self, source, landing):
+        return [
+            pltpu.make_async_remote_copy(
+                src_ref=source(i, self.ranks[i]),
+                dst_ref=landing(i, self.index),
+                send_sem=self.sems[0].at[i],
+                recv_sem=self.sems[1].at[i],
+                device_id=self.targets[i],
+                device_id_type=MESH,
+            )
+            for i in range(self.count - 1)
+        ]
+
+    def start(self, source, landing):
+        for copy in self.copies(source, landing):
+            copy.start()
+
+    def finish(self, source, arrived):
+        sends = self.copies(source, arrived)
+        for i, copy in enumerate(sends):
+            copy.wait_send()
+            pltpu.make_async_remote_copy(
+                src_ref=source(i, self.ranks[i]),
+                dst_ref=arrived(i, self.origins[i]),
+                send_sem=self.sems[0].at[i],
+                recv_sem=self.sems[1].at[i],
+                device_id=self.targets[i],
+                device_id_type=MESH,
+            ).wait_recv()
+
+
+def add_rows(target, own, arrived, count, rows, step):
+    def body(i, carry):
+        at = pl.multiple_of(i * step, step)
+        total = own(at).astype(F32)
+        for r in range(count):
+            total = total + arrived[r, pl.ds(at, step)].astype(F32)
+        target(at, total.astype(BF))
+        return carry
+
+    lax.fori_loop(0, rows // step, body, 0)
+
+
+class Plan:
+    def __init__(self, sizes, channels):
+        self.nx, self.ny = sizes
+        self.inner = 4 if self.nx % 4 == 0 else 1
+        self.outer = self.nx // self.inner
+        self.rows = channels // self.ny
+        self.padded = -(-self.rows // 16) * 16
+        self.full = channels // 128
+        self.tail = channels % 128
+        self.per = 128 // self.tail if self.tail else 1
+        self.groups = -(-27 // self.per) if self.tail else 0
+        total = (27 * self.full + self.groups) * self.padded
+        self.chunk = -(-total // (16 * self.nx)) * 16
+        self.total = self.chunk * self.nx
+        self.used = total
+
+
+def pack_weight_gradient(plan, stage, wide, width):
+    rows, padded = plan.rows, plan.padded
+
+    def piece(e, share, low, high):
+        j, k = e // 3, e % 3
+        value = wide[j, share * rows : (share + 1) * rows, k * width + low : k * width + high]
+        if padded != rows:
+            value = jnp.concatenate([value, jnp.zeros((padded - rows, high - low), F32)], 0)
+        return value
+
+    for share in range(plan.ny):
+        at = 0
+        for e in range(27):
+            for tile in range(plan.full):
+                block = piece(e, share, 128 * tile, 128 * tile + 128)
+                stage[share, at : at + padded] = block.astype(BF)
+                at += padded
+        for g in range(plan.groups):
+            parts = []
+            for e in range(g * plan.per, (g + 1) * plan.per):
+                low = 128 * plan.full
+                parts.append(
+                    piece(e, share, low, low + plan.tail)
+                    if e < 27
+                    else jnp.zeros((padded, plan.tail), F32)
+                )
+            stage[share, at : at + padded] = jnp.concatenate(parts, 1).astype(BF)
+            at += padded
+        if at < plan.total:
+            stage[share, at:] = jnp.zeros((plan.total - at, 128), BF)
+
+
+def unpack_weight_gradient(plan, final, out):
+    rows, padded, tail = plan.rows, plan.padded, plan.tail
+    at = 0
+    for e in range(27):
+        for tile in range(plan.full):
+            out[e, :, 128 * tile : 128 * tile + 128] = final[at : at + padded].astype(F32)[:rows]
+            at += padded
+    for g in range(plan.groups):
+        block = final[at : at + padded].astype(F32)[:rows]
+        for i, e in enumerate(range(g * plan.per, min(27, (g + 1) * plan.per))):
+            out[e, :, 128 * plan.full :] = block[:, i * tail : (i + 1) * tail]
+        at += padded
+
+
+def whole_kernel(
+    sizes, plan, fine, coarse_place, parents, counts, skip, coarse, cot, up_raw, weight_raw,
+    grad_skip, grad_coarse, grad_conv,
+    own, window, acc, turned, up, weight, wide, stage, summed, partial, final,
+    in_y, in_inner, in_outer,
+    face_send, face_recv, edge_send, edge_recv, send_sem, recv_sem,
+    face_send2, face_recv2, edge_send2, edge_recv2, send_sem2, recv_sem2,
+    ring_send, ring_recv,
 ):
     slots, channels, voxels = skip.shape
     width = own.shape[-1]
-    exchange = Exchange(sizes, face_send, face_recv, edge_send, edge_recv, send_sem, recv_sem)
-    exchange.greet()
+    gx, gy = lax.axis_index("gx"), lax.axis_index("gy")
+    first = Exchange(sizes, face_send, face_recv, edge_send, edge_recv, send_sem, recv_sem)
+    second = Exchange(sizes, face_send2, face_recv2, edge_send2, edge_recv2, send_sem2, recv_sem2)
+    inner, outer = plan.inner, plan.outer
+    a, b = lax.rem(gx, inner), lax.div(gx, inner)
+
+    def sems(i):
+        return ring_send.at[i], ring_recv.at[i]
+
+    ring_y = Ring(gy, plan.ny, lambda r: (gx, r), *sems(0))
+    to_inner = lambda r: (b * inner + r, gy)
+    to_outer = lambda r: (r * inner + a, gy)
+    ring_1 = Ring(a, inner, to_inner, *sems(1))
+    ring_2 = Ring(b, outer, to_outer, *sems(2))
+    ring_3 = Ring(b, outer, to_outer, *sems(3))
+    ring_4 = Ring(a, inner, to_inner, *sems(4))
+    others = ring_y.targets + ring_1.targets + ring_2.targets
+    first.greet(others)
+
+    meta = {}
+    for m in range(slots):
+        parent = parents[m]
+        for i in range(3):
+            base = sum(
+                jnp.where(parent == n, coarse_place[n, i], 0) for n in range(coarse.shape[0])
+            )
+            meta[m, i] = fine[m, i]
+            meta[m, 3 + i] = fine[m, i] - 2 * base
+        meta[m, 6] = parent
+        meta[m, 7] = jnp.where(m < counts[0], 1, 0)
+    info = jnp.stack(
+        [
+            jnp.concatenate(
+                [jnp.full((8, width), meta[m, i].astype(F32), F32) for m in range(slots)], 0
+            )
+            for i in range(3)
+        ],
+        0,
+    ).astype(BF)
+
+    up[...] = jnp.zeros_like(up)
+    for k in range(8):
+        up[k * width : k * width + channels, 0:channels] = up_raw[k]
+    weight[...] = jnp.zeros_like(weight)
+    for e in range(27):
+        low = (e % 3) * width
+        weight[e // 3, 0:channels, low : low + channels] = weight_raw[e]
+
     eye = identity(voxels)
-    spread = one_hot(
-        iota((voxels, voxels), 1) == child_row(iota((voxels, voxels), 0))
-    )
+    spread = one_hot(iota((voxels, voxels), 1) == child_row(iota((voxels, voxels), 0)))
     rows = []
     for m in range(slots):
         octant = None
@@ -279,11 +445,11 @@
         total = dot(spread, high) + dot(spread, low) + dot(eye, padded_rows(skip[m], width), NT)
         rows.append((total * meta[m, 7].astype(F32)).reshape(64, 8, width))
     own[...] = jnp.concatenate(rows, 1).astype(BF)
-    exchange.pack(own, info)
-    exchange.await_greetings()
-    exchange.start()
+    first.pack(own, info)
+    first.await_greetings(others)
+    first.start()
     build_centre(window, own, meta, slots)
-    exchange.finish()
+    first.finish()
     build_border(window, own, face_recv, edge_recv, meta, slots)
     acc[...] = jnp.zeros_like(acc)
 
@@ -301,37 +467,67 @@
         value = value * (sigma * (1.0 + pre * (1.0 - sigma))) * meta[m, 7].astype(F32)
         grads.append(value.reshape(64, 8, width))
     grad = jnp.concatenate(grads, 1)
-    grad_pre[...] = grad.astype(BF)
+    own[...] = grad.astype(BF)
+    second.pack(own, info)
+    second.start()
     turned[...] = jnp.transpose(grad.reshape(64 * 8 * slots, width)).astype(BF)
 
-    def outer(j, carry):
-        grad_weight[j] = dot(turned[...], patch(window, j)).astype(BF)
+    def outer_product(j, carry):
+        wide[j] = dot(turned[...], patch(window, j))
         return carry
 
-    lax.fori_loop(0, 9, outer, 0)
-
-
-def backward_kernel(
-    sizes, meta, info, own, up, weight, grad_skip, grad_coarse,
-    window, acc, face_send, face_recv, edge_send, edge_recv, send_sem, recv_sem,
-):
-    slots, channels, voxels = grad_skip.shape
-    width = own.shape[-1]
-    exchange = Exchange(sizes, face_send, face_recv, edge_send, edge_recv, send_sem, recv_sem)
-    exchange.greet()
-    exchange.pack(own, info)
-    exchange.await_greetings()
-    exchange.start()
+    lax.fori_loop(0, 9, outer_product, 0)
+    pack_weight_gradient(plan, stage, wide, width)
+
+    chunk, total, part = plan.chunk, plan.total, plan.chunk * outer
+    span_1 = lambda r: pl.ds(pl.multiple_of(r * part, 16), part)
+    span_2 = lambda r: pl.ds(pl.multiple_of(r * chunk, 16), chunk)
+    span_f = lambda ra, rb: pl.ds(pl.multiple_of((ra * outer + rb) * chunk, 16), chunk)
+    source_y, land_y = (lambda i, r: stage.at[r]), (lambda i, r: in_y.at[i])
+    source_1, land_1 = (lambda i, r: summed.at[span_1(r)]), (lambda i, r: in_inner.at[i])
+    source_2, land_2 = (lambda i, r: partial.at[span_2(r)]), (lambda i, r: in_outer.at[i])
+    source_3, land_3 = (lambda i, r: final.at[span_f(a, b)]), (lambda i, r: final.at[span_f(a, r)])
+    source_4, land_4 = (lambda i, r: final.at[span_1(a)]), (lambda i, r: final.at[span_1(r)])
+
+    def store_to(ref, base):
+        def store(at, value):
+            ref[pl.ds(pl.multiple_of(base + at, 16), value.shape[0])] = value
+        return store
+
+    def load_from(ref, base, step):
+        return lambda at: ref[pl.ds(pl.multiple_of(base + at, 16), step)]
+
+    ring_y.start(source_y, land_y)
     build_centre(window, own, meta, slots)
-    exchange.finish()
-    build_border(window, own, face_recv, edge_recv, meta, slots)
+    ring_y.finish(source_y, land_y)
+    add_rows(
+        store_to(summed, 0), lambda at: stage[gy, pl.ds(at, chunk)], in_y, plan.ny - 1, total, chunk
+    )
+    ring_1.start(source_1, land_1)
+
+    second.finish()
+    build_border(window, own, face_recv2, edge_recv2, meta, slots)
     acc[...] = jnp.zeros_like(acc)
 
-    def conv(j, carry):
-        acc[...] += dot(patch(window, j), weight[j])
+    def conv_back(j, carry):
+        rows = patch(window, j)
+        value = None
+        for k in range(3):
+            term = dot(
+                rows[:, k * width : (k + 1) * width],
+                weight[8 - j, :, (2 - k) * width : (3 - k) * width],
+            )
+            value = term if value is None else value + term
+        acc[...] += value
         return carry
 
-    lax.fori_loop(0, 9, conv, 0)
+    lax.fori_loop(0, 9, conv_back, 0)
+    ring_1.finish(source_1, land_1)
+    add_rows(
+        store_to(partial, 0), load_from(summed, a * part, chunk), in_inner, inner - 1, part, chunk
+    )
+    ring_2.start(source_2, land_2)
+
     all_rows = acc[...].reshape(64, 8 * slots, width)
     gather = one_hot(iota((voxels, voxels), 0) == child_row(iota((voxels, voxels), 1)))
     folded = []
@@ -339,16 +535,27 @@
         rows = all_rows[:, 8 * m : 8 * m + 8].reshape(voxels, width) * meta[m, 7].astype(F32)
         grad_skip[m] = jnp.transpose(rows).astype(BF)[:channels]
         grouped = dot(gather, rows.astype(BF)).astype(BF)
-        grouped = jnp.concatenate([grouped[64 * k : 64 * k + 64] for k in range(8)], 1)
-        folded.append(jnp.transpose(dot(grouped, up[...])).astype(BF))
+        folded.append(jnp.concatenate([grouped[64 * k : 64 * k + 64] for k in range(8)], 1))
+
+    ring_2.finish(source_2, land_2)
+    add_rows(
+        store_to(final, (a * outer + b) * chunk), load_from(partial, b * chunk, 16),
+        in_outer, outer - 1, chunk, 16,
+    )
+    ring_3.start(source_3, land_3)
+    folded = [jnp.transpose(dot(grouped, up[...])).astype(BF) for grouped in folded]
+    ring_3.finish(source_3, land_3)
+    ring_4.start(source_4, land_4)
     for n in range(grad_coarse.shape[0]):
-        total = None
+        value = None
         for m in range(slots):
             column = octant_column(iota((64, voxels), 0), meta, m)
             place = one_hot((iota((64, voxels), 1) == column) & (meta[m, 6] == n))
-            part = dot(folded[m], place)
-            total = part if total is None else total + part
-        grad_coarse[n] = total.astype(BF)[:channels]
+            term = dot(folded[m], place)
+            value = term if value is None else value + term
+        grad_coarse[n] = value.astype(BF)[:channels]
+    ring_4.finish(source_4, land_4)
+    unpack_weight_gradient(plan, final, grad_conv)
 
 
 def exchange_scratch(slots, width):
@@ -368,58 +575,53 @@
 ):
     slots, channels, voxels = skip_feature_rows.shape
     width = -(-channels // 128) * 128
-    extra = width - channels
-    octants = fine_coords - 2 * coarse_coords[parents]
-    occupied = (jnp.arange(slots, dtype=jnp.int32) < counts[0]).astype(jnp.int32)
-    meta = jnp.concatenate([fine_coords, octants, parents[:, None], occupied[:, None]], 1)
-    info = jnp.broadcast_to(
-        jnp.repeat(fine_coords.T.astype(BF), 8, axis=1)[:, :, None], (3, 8 * slots, width)
-    )
-    up = jnp.pad(up_weight, ((0, 0), (0, extra), (0, extra))).reshape(8 * width, width)
-    padded = jnp.pad(conv_weight, ((0, extra), (0, 0), (0, extra)))
-    weight_forward = padded.reshape(width, 9, 3 * width).transpose(1, 0, 2)
-    weight_backward = padded[:, ::-1].transpose(1, 0, 2).reshape(9, 3 * width, width)
+    plan = Plan(sizes, channels)
+    peers = max(plan.ny, plan.inner, plan.outer, 2) - 1
     smem = pl.BlockSpec(memory_space=pltpu.SMEM)
     vmem = pl.BlockSpec(memory_space=pltpu.VMEM)
-    window = pltpu.VMEM((10, 10, 8 * slots, 3 * width), BF)
-    acc = pltpu.VMEM((64 * 8 * slots, width), F32)
-    rows = jax.ShapeDtypeStruct((64, 8 * slots, width), BF)
-    limit = 56 * 1024 * 1024
-    flops = 2 * 27 * slots * voxels * channels * channels
-    grad_pre, grad_weight = pl.pallas_call(
-        functools.partial(forward_kernel, sizes),
-        out_shape=(rows, jax.ShapeDtypeStruct((9, width, 3 * width), BF)),
-        in_specs=[smem] + [vmem] * 6,
-        out_specs=(vmem, vmem),
+    cells = 64 * 8 * slots
+    grad_skip, grad_coarse, grad_conv = pl.pallas_call(
+        functools.partial(whole_kernel, sizes, plan),
+        out_shape=(
+            jax.ShapeDtypeStruct((slots, channels, voxels), BF),
+            jax.ShapeDtypeStruct(coarse_features.shape, BF),
+            jax.ShapeDtypeStruct((27, plan.rows, channels), F32),
+        ),
+        in_specs=[smem] * 4 + [vmem] * 5,
+        out_specs=(vmem, vmem, vmem),
         scratch_shapes=[
-            pltpu.VMEM(rows.shape, BF), window, acc,
-            pltpu.VMEM((width, 64 * 8 * slots), BF),
-        ] + exchange_scratch(slots, width),
+            pltpu.VMEM((64, 8 * slots, width), BF),
+            pltpu.VMEM((10, 10, 8 * slots, 3 * width), BF),
+            pltpu.VMEM((cells, width), F32),
+            pltpu.VMEM((width, cells), BF),
+            pltpu.VMEM((8 * width, width), BF),
+            pltpu.VMEM((9, width, 3 * width), BF),
+            pltpu.VMEM((9, width, 3 * width), F32),
+            pltpu.VMEM((plan.ny, plan.total, 128), BF),
+            pltpu.VMEM((plan.total, 128), BF),
+            pltpu.VMEM((plan.chunk * plan.outer, 128), BF),
+            pltpu.VMEM((plan.total, 128), BF),
+            pltpu.VMEM((max(plan.ny - 1, 1), plan.total, 128), BF),
+            pltpu.VMEM((max(plan.inner - 1, 1), plan.chunk * plan.outer, 128), BF),
+            pltpu.VMEM((max(plan.outer - 1, 1), plan.chunk, 128), BF),
+        ]
+        + exchange_scratch(slots, width)
+        + exchange_scratch(slots, width)
+        + [pltpu.SemaphoreType.DMA((5, peers)), pltpu.SemaphoreType.DMA((5, peers))],
         compiler_params=pltpu.CompilerParams(
-            collective_id=0, has_side_effects=True, vmem_limit_bytes=limit
+            collective_id=0, has_side_effects=True, vmem_limit_bytes=58 * 1024 * 1024
         ),
-        cost_estimate=pl.CostEstimate(flops=2 * flops, bytes_accessed=12 << 20, transcendentals=0),
-        name="forward",
-    )(meta, info, skip_feature_rows, coarse_features, cotangent, up, weight_forward)
-    grad_conv = grad_weight.reshape(9, width, 3, width)[:, :channels, :, :channels]
-    grad_conv = grad_conv.transpose(1, 0, 2, 3).reshape(channels, 27 * channels)
-    grad_conv = lax.psum_scatter(grad_conv, "gy", scatter_dimension=0, tiled=True)
-    grad_conv = lax.psum(grad_conv, "gx").astype(F32)
-    slab = jax.ShapeDtypeStruct((slots, channels, voxels), BF)
-    coarse_slab = jax.ShapeDtypeStruct(coarse_features.shape, BF)
-    grad_skip, grad_coarse = pl.pallas_call(
-        functools.partial(backward_kernel, sizes),
-        out_shape=(slab, coarse_slab),
-        in_specs=[smem] + [vmem] * 4,
-        out_specs=(vmem, vmem),
-        scratch_shapes=[window, acc] + exchange_scratch(slots, width),
-        compiler_params=pltpu.CompilerParams(
-            collective_id=1, has_side_effects=True, vmem_limit_bytes=limit
+        cost_estimate=pl.CostEstimate(
+            flops=6 * 27 * slots * voxels * channels * channels,
+            bytes_accessed=12 << 20, transcendentals=0,
         ),
-        cost_estimate=pl.CostEstimate(flops=8 * flops, bytes_accessed=64 << 20, transcendentals=0),
-        name="backward",
-    )(meta, info, grad_pre, up, weight_backward)
-    return (grad_skip, grad_coarse, grad_conv.reshape(grad_conv.shape[0], 27, channels))
+        name="whole",
+    )(
+        fine_coords, coarse_coords, parents, counts,
+        skip_feature_rows, coarse_features, cotangent, up_weight,
+        conv_weight.transpose(1, 0, 2),
+    )
+    return (grad_skip, grad_coarse, grad_conv.transpose(1, 0, 2))
 
 
 def solution(mesh):

time: 213 us -> 79.9 us (0.38)
  waiting for transfers between devices: 105 us -> 0 us
  local copies, waits for them, and re-layouts: 42.5 us -> 7.07 us
  Pallas kernels: 46.4 us -> 71.3 us
  between operations: 14.8 us -> 1.29 us
  other arithmetic: 3.3 us -> 0 us
    psum x1 -> x0, waiting for transfers between devices: 101 us -> none  [local(): grad_conv = lax.psum(grad_conv, 'gx').astype(F32)]
    pallas_call x2 -> x1, Pallas kernels: 46.4 us -> 71.3 us  [local(): pl.pallas_call(functools.partial(whole_kernel, sizes, plan), out_shape=(j...]
    unnamed x16 -> x3, local copies, waits for them, and re-layouts: 15.7 us -> 7.07 us
    transpose x2 -> x0, local copies, waits for them, and re-layouts: 7.76 us -> none  [local(): padded[:, ::-1].transpose(1, 0, 2).reshape(9, 3 * width, width)]
    pallas_call x1 -> x0, local copies, waits for them, and re-layouts: 5.73 us -> none  [local(): pl.pallas_call(functools.partial(forward_kernel, sizes), out_shape=(rows,...]
    unnamed x3 -> x0, waiting for transfers between devices: 3.58 us -> none
    reshape x1 -> x0, local copies, waits for them, and re-layouts: 3.55 us -> none  [local(): weight_forward = padded.reshape(width, 9, 3 * width).transpose(1, 0, 2)]
    slice x1 -> x0, local copies, waits for them, and re-layouts: 3.54 us -> none  [local(): grad_weight.reshape(9, width, 3, width)[:, :channels, :, :channels]]
  transfers between devices with their start and end apart: 2 -> 0, of which waited for: 2 -> 0; matrix products, arithmetic and copies ran while one was open for 4% -> 0% of each run, Pallas kernels for 9% -> 0%
where the time goes in v2:
time: 79.9 us; the launch traced here: 79.7 us
  Pallas kernels  71.3 us (89%)
  local copies, waits for them, and re-layouts  7.07 us (9%)
  between operations  1.29 us (2%)
    pallas_call x1, Pallas kernels, local(): pl.pallas_call(functools.partial(whole_kernel, sizes, plan), out_shape=(j...  71.3 us
    unnamed x3, local copies, waits for them, and re-layouts  7.07 us

profile of v2, /device:TPU:0, one launch (start us, length us, event | category | flops | bytes accessed | tf_op | source)
XLA Modules:
  0.0 79.7 jit_solution(8797193441393868154)
XLA Ops:
  1.3 71.3 %whole.1 = (bf16[2,192,512]{2,1,0:T(8,128)(2,1)}, bf16[2,192,512]{2,1,0:T(8,128)(2,1)}, f32[27,96,192]{2,1,0:T(8,128)}) custom-call(s32[2,3]{1,0:T(2,128)} %fine.1, s32[2,3]{1,0:T(2,128)} %coarse_place.1, s32[2]{0:T(128)} %parents.1, s32[1]{0:T(128)S(6)} %copy.15.counts, bf16[2,192,512]{2,1,0:T(8,128)(2,1)} %skip.1, bf16[2,192,512]{2,1,0:T(8,128)(2,1)} %coarse.1, ...), custom_call_target="tpu_custom_call" | custom-call | flops 6115295232 | bytes 12582912 | tf_op jit(solution)/shard_map/whole/pallas_call | solution.py:583
  72.6 1.8 %copy.16 = bf16[2,192,512]{2,1,0:T(8,128)(2,1)} copy(bf16[2,192,512]{2,1,0:T(8,128)(2,1)} %get-tuple-element.12) | data formatting | bytes 786432
  74.4 1.8 %copy.17 = bf16[2,192,512]{2,1,0:T(8,128)(2,1)} copy(bf16[2,192,512]{2,1,0:T(8,128)(2,1)} %get-tuple-element.13) | data formatting | bytes 786432
  76.1 3.5 %copy.18 = f32[96,27,192]{2,0,1:T(8,128)} copy(f32[96,27,192]{2,0,1:T(8,128)} %bitcast.2) | data formatting | bytes 3981312

commit v3 on v2

--- a/solution.py
+++ b/solution.py
@@ -306,6 +306,80 @@
     lax.fori_loop(0, rows // step, body, 0)
 
 
+def store_to(ref, base):
+    def store(at, value):
+        ref[pl.ds(pl.multiple_of(base + at, 16), value.shape[0])] = value
+
+    return store
+
+
+def load_from(ref, base, step):
+    return lambda at: ref[pl.ds(pl.multiple_of(base + at, 16), step)]
+
+
+class Part:
+    def __init__(self, order, chunk, base, sems, summed, partial, final, arrivals):
+        (i, count, to_one), (j, others, to_two) = order
+        self.i, self.j, self.chunk, self.base = i, j, chunk, base
+        self.summed, self.partial, self.final = summed, partial, final
+        self.arrivals = arrivals
+        self.part = part = chunk * others
+        self.mine = base + (i * others + j) * chunk
+        self.rings = [
+            Ring(i, count, to_one, *sems[0]),
+            Ring(j, others, to_two, *sems[1]),
+            Ring(j, others, to_two, *sems[2]),
+            Ring(i, count, to_one, *sems[3]),
+        ]
+        wide = lambda r: pl.ds(pl.multiple_of(base + r * part, 16), part)
+        thin = lambda r: pl.ds(pl.multiple_of(r * chunk, 16), chunk)
+        cell = lambda r: pl.ds(pl.multiple_of(base + (i * others + r) * chunk, 16), chunk)
+        self.source = [
+            lambda n, r: summed.at[wide(r)],
+            lambda n, r: partial.at[thin(r)],
+            lambda n, r: final.at[cell(j)],
+            lambda n, r: final.at[wide(i)],
+        ]
+        self.land = [
+            lambda n, r: arrivals[0].at[n],
+            lambda n, r: arrivals[1].at[n],
+            lambda n, r: final.at[cell(r)],
+            lambda n, r: final.at[wide(r)],
+        ]
+
+    def begin(self, n):
+        self.rings[n].start(self.source[n], self.land[n])
+
+    def end(self, n):
+        self.rings[n].finish(self.source[n], self.land[n])
+
+    def start_first(self):
+        self.begin(0)
+
+    def start_second(self):
+        self.end(0)
+        add_rows(
+            store_to(self.partial, 0), load_from(self.summed, self.base + self.i * self.part, self.chunk),
+            self.arrivals[0], self.rings[0].count - 1, self.part, self.chunk,
+        )
+        self.begin(1)
+
+    def start_third(self):
+        self.end(1)
+        add_rows(
+            store_to(self.final, self.mine), load_from(self.partial, self.j * self.chunk, 16),
+            self.arrivals[1], self.rings[1].count - 1, self.chunk, 16,
+        )
+        self.begin(2)
+
+    def start_fourth(self):
+        self.end(2)
+        self.begin(3)
+
+    def finish(self):
+        self.end(3)
+
+
 class Plan:
     def __init__(self, sizes, channels):
         self.nx, self.ny = sizes
@@ -320,7 +394,8 @@
         total = (27 * self.full + self.groups) * self.padded
         self.chunk = -(-total // (16 * self.nx)) * 16
         self.total = self.chunk * self.nx
-        self.used = total
+        across = self.chunk // 48 * 16 if min(self.inner, self.outer) > 1 else 0
+        self.chunks = [self.chunk - across] + ([across] if across else [])
 
 
 def pack_weight_gradient(plan, stage, wide, width):
@@ -371,9 +446,9 @@
 
 def whole_kernel(
     sizes, plan, fine, coarse_place, parents, counts, skip, coarse, cot, up_raw, weight_raw,
-    grad_skip, grad_coarse, grad_conv,
-    own, window, acc, turned, up, weight, wide, stage, summed, partial, final,
-    in_y, in_inner, in_outer,
+    grad_skip, grad_coarse, grad_rows,
+    own, window, acc, turned, up, weight, fetched, held, wide, stage, summed, partial, final,
+    in_y, arrivals, fetch_sem,
     face_send, face_recv, edge_send, edge_recv, send_sem, recv_sem,
     face_send2, face_recv2, edge_send2, edge_recv2, send_sem2, recv_sem2,
     ring_send, ring_recv,
@@ -392,12 +467,23 @@
     ring_y = Ring(gy, plan.ny, lambda r: (gx, r), *sems(0))
     to_inner = lambda r: (b * inner + r, gy)
     to_outer = lambda r: (r * inner + a, gy)
-    ring_1 = Ring(a, inner, to_inner, *sems(1))
-    ring_2 = Ring(b, outer, to_outer, *sems(2))
-    ring_3 = Ring(b, outer, to_outer, *sems(3))
-    ring_4 = Ring(a, inner, to_inner, *sems(4))
-    others = ring_y.targets + ring_1.targets + ring_2.targets
+    groups = ((a, inner, to_inner), (b, outer, to_outer))
+    base, parts = 0, []
+    for number, chunk in enumerate(plan.chunks):
+        order = groups if number == 0 else groups[::-1]
+        parts.append(
+            Part(order, chunk, base, [sems(1 + 4 * number + i) for i in range(4)],
+                 summed, partial[number], final, arrivals[2 * number : 2 * number + 2])
+        )
+        base += chunk * plan.nx
+    others = ring_y.targets + parts[0].rings[0].targets + parts[0].rings[1].targets
     first.greet(others)
+    fetches = [
+        pltpu.make_async_copy(weight_raw, fetched, fetch_sem.at[0]),
+        pltpu.make_async_copy(cot, held, fetch_sem.at[1]),
+    ]
+    for fetch in fetches:
+        fetch.start()
 
     meta = {}
     for m in range(slots):
@@ -423,19 +509,14 @@
     up[...] = jnp.zeros_like(up)
     for k in range(8):
         up[k * width : k * width + channels, 0:channels] = up_raw[k]
-    weight[...] = jnp.zeros_like(weight)
-    for e in range(27):
-        low = (e % 3) * width
-        weight[e // 3, 0:channels, low : low + channels] = weight_raw[e]
-
     eye = identity(voxels)
-    spread = one_hot(iota((voxels, voxels), 1) == child_row(iota((voxels, voxels), 0)))
+    spread = one_hot(iota((voxels, voxels), 1) == child_row(iota((voxels, 1), 0)))
     rows = []
     for m in range(slots):
         octant = None
-        column = octant_column(iota((64, voxels), 0), meta, m)
+        column = octant_column(iota((64, 1), 0), meta, m)
         for n in range(coarse.shape[0]):
-            pick = one_hot((iota((64, voxels), 1) == column) & (meta[m, 6] == n))
+            pick = one_hot(iota((64, voxels), 1) == jnp.where(meta[m, 6] == n, column, -1))
             part = dot(pick, padded_rows(coarse[n], width), NT)
             octant = part if octant is None else octant + part
         lifted = dot(octant.astype(BF), up[...], NT)
@@ -448,6 +529,11 @@
     first.pack(own, info)
     first.await_greetings(others)
     first.start()
+    weight[...] = jnp.zeros_like(weight)
+    fetches[0].wait()
+    for e in range(27):
+        low = (e % 3) * width
+        weight[e // 3, 0:channels, low : low + channels] = fetched[e]
     build_centre(window, own, meta, slots)
     first.finish()
     build_border(window, own, face_recv, edge_recv, meta, slots)
@@ -460,10 +546,11 @@
     lax.fori_loop(0, 9, conv, 0)
     pre_all = acc[...].reshape(64, 8 * slots, width)
     grads = []
+    fetches[1].wait()
     for m in range(slots):
         pre = pre_all[:, 8 * m : 8 * m + 8].reshape(voxels, width)
         sigma = 1.0 / (1.0 + jnp.exp(-pre))
-        value = dot(eye, padded_rows(cot[m], width), NT)
+        value = dot(eye, padded_rows(held[m], width), NT)
         value = value * (sigma * (1.0 + pre * (1.0 - sigma))) * meta[m, 7].astype(F32)
         grads.append(value.reshape(64, 8, width))
     grad = jnp.concatenate(grads, 1)
@@ -479,31 +566,16 @@
     lax.fori_loop(0, 9, outer_product, 0)
     pack_weight_gradient(plan, stage, wide, width)
 
-    chunk, total, part = plan.chunk, plan.total, plan.chunk * outer
-    span_1 = lambda r: pl.ds(pl.multiple_of(r * part, 16), part)
-    span_2 = lambda r: pl.ds(pl.multiple_of(r * chunk, 16), chunk)
-    span_f = lambda ra, rb: pl.ds(pl.multiple_of((ra * outer + rb) * chunk, 16), chunk)
     source_y, land_y = (lambda i, r: stage.at[r]), (lambda i, r: in_y.at[i])
-    source_1, land_1 = (lambda i, r: summed.at[span_1(r)]), (lambda i, r: in_inner.at[i])
-    source_2, land_2 = (lambda i, r: partial.at[span_2(r)]), (lambda i, r: in_outer.at[i])
-    source_3, land_3 = (lambda i, r: final.at[span_f(a, b)]), (lambda i, r: final.at[span_f(a, r)])
-    source_4, land_4 = (lambda i, r: final.at[span_1(a)]), (lambda i, r: final.at[span_1(r)])
-
-    def store_to(ref, base):
-        def store(at, value):
-            ref[pl.ds(pl.multiple_of(base + at, 16), value.shape[0])] = value
-        return store
-
-    def load_from(ref, base, step):
-        return lambda at: ref[pl.ds(pl.multiple_of(base + at, 16), step)]
-
     ring_y.start(source_y, land_y)
     build_centre(window, own, meta, slots)
     ring_y.finish(source_y, land_y)
     add_rows(
-        store_to(summed, 0), lambda at: stage[gy, pl.ds(at, chunk)], in_y, plan.ny - 1, total, chunk
+        store_to(summed, 0), lambda at: stage[gy, pl.ds(at, plan.chunk)],
+        in_y, plan.ny - 1, plan.total, plan.chunk,
     )
-    ring_1.start(source_1, land_1)
+    for part in parts:
+        part.start_first()
 
     second.finish()
     build_border(window, own, face_recv2, edge_recv2, meta, slots)
@@ -522,14 +594,11 @@
         return carry
 
     lax.fori_loop(0, 9, conv_back, 0)
-    ring_1.finish(source_1, land_1)
-    add_rows(
-        store_to(partial, 0), load_from(summed, a * part, chunk), in_inner, inner - 1, part, chunk
-    )
-    ring_2.start(source_2, land_2)
+    for part in parts:
+        part.start_second()
 
     all_rows = acc[...].reshape(64, 8 * slots, width)
-    gather = one_hot(iota((voxels, voxels), 0) == child_row(iota((voxels, voxels), 1)))
+    gather = one_hot(iota((voxels, voxels), 0) == child_row(iota((1, voxels), 1)))
     folded = []
     for m in range(slots):
         rows = all_rows[:, 8 * m : 8 * m + 8].reshape(voxels, width) * meta[m, 7].astype(F32)
@@ -537,25 +606,28 @@
         grouped = dot(gather, rows.astype(BF)).astype(BF)
         folded.append(jnp.concatenate([grouped[64 * k : 64 * k + 64] for k in range(8)], 1))
 
-    ring_2.finish(source_2, land_2)
-    add_rows(
-        store_to(final, (a * outer + b) * chunk), load_from(partial, b * chunk, 16),
-        in_outer, outer - 1, chunk, 16,
-    )
-    ring_3.start(source_3, land_3)
+    for part in parts:
+        part.start_third()
     folded = [jnp.transpose(dot(grouped, up[...])).astype(BF) for grouped in folded]
-    ring_3.finish(source_3, land_3)
-    ring_4.start(source_4, land_4)
+    for part in parts:
+        part.start_fourth()
     for n in range(grad_coarse.shape[0]):
         value = None
         for m in range(slots):
-            column = octant_column(iota((64, voxels), 0), meta, m)
-            place = one_hot((iota((64, voxels), 1) == column) & (meta[m, 6] == n))
+            column = octant_column(iota((64, 1), 0), meta, m)
+            place = one_hot(iota((64, voxels), 1) == jnp.where(meta[m, 6] == n, column, -1))
             term = dot(folded[m], place)
             value = term if value is None else value + term
         grad_coarse[n] = value.astype(BF)[:channels]
-    ring_4.finish(source_4, land_4)
-    unpack_weight_gradient(plan, final, grad_conv)
+    for part in parts:
+        part.finish()
+    grad_rows[...] = final[...]
+
+
+def output_kernel(plan, skip_in, coarse_in, rows_in, skip_out, coarse_out, conv_out):
+    skip_out[...] = skip_in[...]
+    coarse_out[...] = coarse_in[...]
+    unpack_weight_gradient(plan, rows_in, conv_out)
 
 
 def exchange_scratch(slots, width):
@@ -579,15 +651,22 @@
     peers = max(plan.ny, plan.inner, plan.outer, 2) - 1
     smem = pl.BlockSpec(memory_space=pltpu.SMEM)
     vmem = pl.BlockSpec(memory_space=pltpu.VMEM)
+    anywhere = pl.BlockSpec(memory_space=pl.ANY)
     cells = 64 * 8 * slots
-    grad_skip, grad_coarse, grad_conv = pl.pallas_call(
+    partials, arrivals = [], []
+    for number, chunk in enumerate(plan.chunks):
+        sides = (plan.inner, plan.outer) if number == 0 else (plan.outer, plan.inner)
+        partials.append(pltpu.VMEM((chunk * sides[1], 128), BF))
+        arrivals.append(pltpu.VMEM((max(sides[0] - 1, 1), chunk * sides[1], 128), BF))
+        arrivals.append(pltpu.VMEM((max(sides[1] - 1, 1), chunk, 128), BF))
+    grad_skip, grad_coarse, grad_rows = pl.pallas_call(
         functools.partial(whole_kernel, sizes, plan),
         out_shape=(
             jax.ShapeDtypeStruct((slots, channels, voxels), BF),
             jax.ShapeDtypeStruct(coarse_features.shape, BF),
-            jax.ShapeDtypeStruct((27, plan.rows, channels), F32),
+            jax.ShapeDtypeStruct((plan.total, 128), BF),
         ),
-        in_specs=[smem] * 4 + [vmem] * 5,
+        in_specs=[smem] * 4 + [vmem, vmem, anywhere, vmem, anywhere],
         out_specs=(vmem, vmem, vmem),
         scratch_shapes=[
             pltpu.VMEM((64, 8 * slots, width), BF),
@@ -596,20 +675,22 @@
             pltpu.VMEM((width, cells), BF),
             pltpu.VMEM((8 * width, width), BF),
             pltpu.VMEM((9, width, 3 * width), BF),
+            pltpu.VMEM((27, channels, channels), BF),
+            pltpu.VMEM((slots, channels, voxels), BF),
             pltpu.VMEM((9, width, 3 * width), F32),
             pltpu.VMEM((plan.ny, plan.total, 128), BF),
             pltpu.VMEM((plan.total, 128), BF),
-            pltpu.VMEM((plan.chunk * plan.outer, 128), BF),
+            tuple(partials),
             pltpu.VMEM((plan.total, 128), BF),
             pltpu.VMEM((max(plan.ny - 1, 1), plan.total, 128), BF),
-            pltpu.VMEM((max(plan.inner - 1, 1), plan.chunk * plan.outer, 128), BF),
-            pltpu.VMEM((max(plan.outer - 1, 1), plan.chunk, 128), BF),
+            tuple(arrivals),
+            pltpu.SemaphoreType.DMA((2,)),
         ]
         + exchange_scratch(slots, width)
         + exchange_scratch(slots, width)
-        + [pltpu.SemaphoreType.DMA((5, peers)), pltpu.SemaphoreType.DMA((5, peers))],
+        + [pltpu.SemaphoreType.DMA((9, peers)), pltpu.SemaphoreType.DMA((9, peers))],
         compiler_params=pltpu.CompilerParams(
-            collective_id=0, has_side_effects=True, vmem_limit_bytes=58 * 1024 * 1024
+            collective_id=0, has_side_effects=True, vmem_limit_bytes=60 * 1024 * 1024
         ),
         cost_estimate=pl.CostEstimate(
             flops=6 * 27 * slots * voxels * channels * channels,
@@ -621,6 +702,18 @@
         skip_feature_rows, coarse_features, cotangent, up_weight,
         conv_weight.transpose(1, 0, 2),
     )
+    grad_skip, grad_coarse, grad_conv = pl.pallas_call(
+        functools.partial(output_kernel, plan),
+        out_shape=(
+            jax.ShapeDtypeStruct(grad_skip.shape, BF),
+            jax.ShapeDtypeStruct(grad_coarse.shape, BF),
+            jax.ShapeDtypeStruct((27, plan.rows, channels), F32),
+        ),
+        in_specs=[vmem] * 3,
+        out_specs=(vmem, vmem, vmem),
+        compiler_params=pltpu.CompilerParams(vmem_limit_bytes=60 * 1024 * 1024),
+        name="outputs",
+    )(grad_skip, grad_coarse, grad_rows)
     return (grad_skip, grad_coarse, grad_conv.transpose(1, 0, 2))
 
 

time: 79.9 us -> 64.5 us (0.81)
  Pallas kernels: 71.3 us -> 63 us
  local copies, waits for them, and re-layouts: 7.07 us -> 0 us
    pallas_call x1, Pallas kernels: 71.3 us -> 59.7 us  [local(): pl.pallas_call(functools.partial(whole_kernel, sizes, plan), out_shape=(j...]
    unnamed x3 -> x0, local copies, waits for them, and re-layouts: 7.07 us -> none
    pallas_call x0 -> x1, Pallas kernels: none -> 3.34 us  [local(): pl.pallas_call(functools.partial(output_kernel, plan), out_shape=(jax.Sha...]
where the time goes in v3:
time: 64.5 us; the launch traced here: 64.3 us
  Pallas kernels  63 us (98%)
  between operations  1.29 us (2%)
    pallas_call x1, Pallas kernels, local(): pl.pallas_call(functools.partial(whole_kernel, sizes, plan), out_shape=(j...  59.7 us
    pallas_call x1, Pallas kernels, local(): pl.pallas_call(functools.partial(output_kernel, plan), out_shape=(jax.Sha...  3.34 us

profile of v3, /device:TPU:0, one launch (start us, length us, event | category | flops | bytes accessed | tf_op | source)
XLA Modules:
  0.0 64.3 jit_solution(12327793740385650711)
XLA Ops:
  1.3 59.7 %whole.1 = (bf16[2,192,512]{2,1,0:T(8,128)(2,1)}, bf16[2,192,512]{2,1,0:T(8,128)(2,1)}, bf16[4096,128]{1,0:T(8,128)(2,1)}) custom-call(s32[2,3]{1,0:T(2,128)} %fine.1, s32[2,3]{1,0:T(2,128)} %coarse_place.1, s32[2]{0:T(128)} %parents.1, s32[1]{0:T(128)S(6)} %copy.12.counts, bf16[2,192,512]{2,1,0:T(8,128)(2,1)} %skip.1, bf16[2,192,512]{2,1,0:T(8,128)(2,1)} %coarse.1, ...), custom_call_target="tpu_custom_call" | custom-call | flops 6115295232 | bytes 12582912 | tf_op jit(solution)/shard_map/whole/pallas_call | solution.py:662
  61.0 3.3 %outputs.1 = (bf16[2,192,512]{2,1,0:T(8,128)(2,1)}, bf16[2,192,512]{2,1,0:T(8,128)(2,1)}, f32[27,96,192]{2,1,0:T(8,128)}) custom-call(bf16[2,192,512]{2,1,0:T(8,128)(2,1)} %get-tuple-element.9.skip_in, bf16[2,192,512]{2,1,0:T(8,128)(2,1)} %get-tuple-element.10.coarse_in, bf16[4096,128]{1,0:T(8,128)(2,1)} %get-tuple-element.11.rows_in), custom_call_target="tpu_custom_call" | custom-call | tf_op jit(solution)/shard_map/outputs/pallas_call | solution.py:705

commit v4 on v3

--- a/solution.py
+++ b/solution.py
@@ -140,23 +140,20 @@
     below = jnp.where(same & (step == -1.0), 1.0, 0.0)
     above = jnp.where(same & (step == 1.0), 1.0, 0.0)
     level = iota(here.shape, 0)
-    return jnp.where(level == 0, below, here), here, jnp.where(level == 7, above, here)
-
-
-def shifted(block):
-    width = block.shape[-1]
-    flat = block.reshape(-1, 8, width)
-    down = pltpu.roll(flat, 1, 1).reshape(block.shape)
-    up = pltpu.roll(flat, 7, 1).reshape(block.shape)
-    return down, block, up
+    return jnp.where(level == 7, below, here), here, jnp.where(level == 0, above, here)
+
+
+def rolled(block, step):
+    flat = block.reshape(-1, 8, block.shape[-1])
+    return pltpu.roll(flat, step, 1).reshape(block.shape)
 
 
 def sum_sources(sources):
     total = None
     for block, weights in sources:
-        terms = [part * weight for part, weight in zip(shifted(block), weights)]
+        terms = [block if weight is None else block * weight for weight in weights]
         total = terms if total is None else [a + b for a, b in zip(total, terms)]
-    return total
+    return rolled(total[0], 1), total[1], rolled(total[2], 7)
 
 
 def put(window, at_x, at_y, per_slot):
@@ -181,7 +178,7 @@
     width = own.shape[-1]
     ones = jnp.ones((8, width), F32)
     level = iota((8, width), 0)
-    self_weights = (jnp.where(level == 0, 0.0, ones), ones, jnp.where(level == 7, 0.0, ones))
+    self_weights = (jnp.where(level == 7, 0.0, ones), None, jnp.where(level == 0, 0.0, ones))
     other = [
         [(s, weights_of(own_place(meta, s, width), meta, m, 0, 0)) for s in range(slots) if s != m]
         for m in range(slots)
@@ -593,9 +590,12 @@
         acc[...] += value
         return carry
 
-    lax.fori_loop(0, 9, conv_back, 0)
+    lax.fori_loop(0, 4, conv_back, 0)
     for part in parts:
         part.start_second()
+    lax.fori_loop(4, 9, conv_back, 0)
+    for part in parts:
+        part.start_third()
 
     all_rows = acc[...].reshape(64, 8 * slots, width)
     gather = one_hot(iota((voxels, voxels), 0) == child_row(iota((1, voxels), 1)))
@@ -607,10 +607,8 @@
         folded.append(jnp.concatenate([grouped[64 * k : 64 * k + 64] for k in range(8)], 1))
 
     for part in parts:
-        part.start_third()
+        part.start_fourth()
     folded = [jnp.transpose(dot(grouped, up[...])).astype(BF) for grouped in folded]
-    for part in parts:
-        part.start_fourth()
     for n in range(grad_coarse.shape[0]):
         value = None
         for m in range(slots):

time: 64.5 us -> 64.4 us (level)
  no operation moved by 1% of the time
where the time goes in v4:
time: 64.4 us; the launch traced here: 64.2 us
  Pallas kernels  63 us (98%)
  between operations  1.29 us (2%)
    pallas_call x1, Pallas kernels, local(): pl.pallas_call(functools.partial(whole_kernel, sizes, plan), out_shape=(j...  59.6 us
    pallas_call x1, Pallas kernels, local(): pl.pallas_call(functools.partial(output_kernel, plan), out_shape=(jax.Sha...  3.34 us

profile of v4, /device:TPU:0, one launch (start us, length us, event | category | flops | bytes accessed | tf_op | source)
XLA Modules:
  0.0 64.2 jit_solution(14632940046196600329)
XLA Ops:
  1.3 59.6 %whole.1 = (bf16[2,192,512]{2,1,0:T(8,128)(2,1)}, bf16[2,192,512]{2,1,0:T(8,128)(2,1)}, bf16[4096,128]{1,0:T(8,128)(2,1)}) custom-call(s32[2,3]{1,0:T(2,128)} %fine.1, s32[2,3]{1,0:T(2,128)} %coarse_place.1, s32[2]{0:T(128)} %parents.1, s32[1]{0:T(128)S(6)} %copy.12.counts, bf16[2,192,512]{2,1,0:T(8,128)(2,1)} %skip.1, bf16[2,192,512]{2,1,0:T(8,128)(2,1)} %coarse.1, ...), custom_call_target="tpu_custom_call" | custom-call | flops 6115295232 | bytes 12582912 | tf_op jit(solution)/shard_map/whole/pallas_call | solution.py:660
  60.9 3.3 %outputs.1 = (bf16[2,192,512]{2,1,0:T(8,128)(2,1)}, bf16[2,192,512]{2,1,0:T(8,128)(2,1)}, f32[27,96,192]{2,1,0:T(8,128)}) custom-call(bf16[2,192,512]{2,1,0:T(8,128)(2,1)} %get-tuple-element.9.skip_in, bf16[2,192,512]{2,1,0:T(8,128)(2,1)} %get-tuple-element.10.coarse_in, bf16[4096,128]{1,0:T(8,128)(2,1)} %get-tuple-element.11.rows_in), custom_call_target="tpu_custom_call" | custom-call | tf_op jit(solution)/shard_map/outputs/pallas_call | solution.py:703

commit v5 on v4

--- a/solution.py
+++ b/solution.py
@@ -291,16 +291,16 @@
             ).wait_recv()
 
 
-def add_rows(target, own, arrived, count, rows, step):
+def add_rows(target, own, arrived, count, low, high, step):
     def body(i, carry):
-        at = pl.multiple_of(i * step, step)
+        at = pl.multiple_of(low + i * step, 16)
         total = own(at).astype(F32)
         for r in range(count):
             total = total + arrived[r, pl.ds(at, step)].astype(F32)
         target(at, total.astype(BF))
         return carry
 
-    lax.fori_loop(0, rows // step, body, 0)
+    lax.fori_loop(0, (high - low) // step, body, 0)
 
 
 def store_to(ref, base):
@@ -357,7 +357,7 @@
         self.end(0)
         add_rows(
             store_to(self.partial, 0), load_from(self.summed, self.base + self.i * self.part, self.chunk),
-            self.arrivals[0], self.rings[0].count - 1, self.part, self.chunk,
+            self.arrivals[0], self.rings[0].count - 1, 0, self.part, self.chunk,
         )
         self.begin(1)
 
@@ -365,7 +365,7 @@
         self.end(1)
         add_rows(
             store_to(self.final, self.mine), load_from(self.partial, self.j * self.chunk, 16),
-            self.arrivals[1], self.rings[1].count - 1, self.chunk, 16,
+            self.arrivals[1], self.rings[1].count - 1, 0, self.chunk, 16,
         )
         self.begin(2)
 
@@ -391,11 +391,29 @@
         total = (27 * self.full + self.groups) * self.padded
         self.chunk = -(-total // (16 * self.nx)) * 16
         self.total = self.chunk * self.nx
+        self.used = total
+        self.blocks, at, starts = [], 0, {}
+        for first in range(0, 27, self.per):
+            es = list(range(first, min(27, first + self.per)))
+            starts[first] = at
+            for e in es:
+                for tile in range(self.full):
+                    self.blocks.append(([e], tile, at))
+                    at += self.padded
+            if self.tail:
+                self.blocks.append((es, None, at))
+                at += self.padded
+        self.steps = (0, 4, 6, 9)
+        ends = [0]
+        for bound in self.steps[1:-1]:
+            ends.append(max(row for e, row in starts.items() if e <= 3 * bound))
+        ends.append(self.total)
+        self.spans = list(zip(ends[:-1], ends[1:]))
         across = self.chunk // 48 * 16 if min(self.inner, self.outer) > 1 else 0
         self.chunks = [self.chunk - across] + ([across] if across else [])
 
 
-def pack_weight_gradient(plan, stage, wide, width):
+def pack_weight_gradient(plan, stage, wide, width, span):
     rows, padded = plan.rows, plan.padded
 
     def piece(e, share, low, high):
@@ -405,40 +423,34 @@
             value = jnp.concatenate([value, jnp.zeros((padded - rows, high - low), F32)], 0)
         return value
 
+    low, high = span
     for share in range(plan.ny):
-        at = 0
-        for e in range(27):
-            for tile in range(plan.full):
-                block = piece(e, share, 128 * tile, 128 * tile + 128)
-                stage[share, at : at + padded] = block.astype(BF)
-                at += padded
-        for g in range(plan.groups):
-            parts = []
-            for e in range(g * plan.per, (g + 1) * plan.per):
-                low = 128 * plan.full
-                parts.append(
-                    piece(e, share, low, low + plan.tail)
-                    if e < 27
-                    else jnp.zeros((padded, plan.tail), F32)
-                )
-            stage[share, at : at + padded] = jnp.concatenate(parts, 1).astype(BF)
-            at += padded
-        if at < plan.total:
-            stage[share, at:] = jnp.zeros((plan.total - at, 128), BF)
+        for es, tile, at in plan.blocks:
+            if not low <= at < high:
+                continue
+            if tile is not None:
+                block = piece(es[0], share, 128 * tile, 128 * tile + 128)
+            else:
+                base = 128 * plan.full
+                parts = [piece(e, share, base, base + plan.tail) for e in es]
+                left = 128 - plan.tail * len(es)
+                if left:
+                    parts.append(jnp.zeros((padded, left), F32))
+                block = jnp.concatenate(parts, 1)
+            stage[share, at : at + padded] = block.astype(BF)
+        if high == plan.total and plan.used < plan.total:
+            stage[share, plan.used :] = jnp.zeros((plan.total - plan.used, 128), BF)
 
 
 def unpack_weight_gradient(plan, final, out):
     rows, padded, tail = plan.rows, plan.padded, plan.tail
-    at = 0
-    for e in range(27):
-        for tile in range(plan.full):
-            out[e, :, 128 * tile : 128 * tile + 128] = final[at : at + padded].astype(F32)[:rows]
-            at += padded
-    for g in range(plan.groups):
+    for es, tile, at in plan.blocks:
         block = final[at : at + padded].astype(F32)[:rows]
-        for i, e in enumerate(range(g * plan.per, min(27, (g + 1) * plan.per))):
-            out[e, :, 128 * plan.full :] = block[:, i * tail : (i + 1) * tail]
-        at += padded
+        if tile is not None:
+            out[es[0], :, 128 * tile : 128 * tile + 128] = block
+        else:
+            for i, e in enumerate(es):
+                out[e, :, 128 * plan.full :] = block[:, i * tail : (i + 1) * tail]
 
 
 def whole_kernel(
@@ -461,7 +473,7 @@
     def sems(i):
         return ring_send.at[i], ring_recv.at[i]
 
-    ring_y = Ring(gy, plan.ny, lambda r: (gx, r), *sems(0))
+    rings_y = [Ring(gy, plan.ny, lambda r: (gx, r), *sems(i)) for i in (0, 9, 10)]
     to_inner = lambda r: (b * inner + r, gy)
     to_outer = lambda r: (r * inner + a, gy)
     groups = ((a, inner, to_inner), (b, outer, to_outer))
@@ -473,7 +485,7 @@
                  summed, partial[number], final, arrivals[2 * number : 2 * number + 2])
         )
         base += chunk * plan.nx
-    others = ring_y.targets + parts[0].rings[0].targets + parts[0].rings[1].targets
+    others = rings_y[0].targets + parts[0].rings[0].targets + parts[0].rings[1].targets
     first.greet(others)
     fetches = [
         pltpu.make_async_copy(weight_raw, fetched, fetch_sem.at[0]),
@@ -560,18 +572,23 @@
         wide[j] = dot(turned[...], patch(window, j))
         return carry
 
-    lax.fori_loop(0, 9, outer_product, 0)
-    pack_weight_gradient(plan, stage, wide, width)
-
-    source_y, land_y = (lambda i, r: stage.at[r]), (lambda i, r: in_y.at[i])
-    ring_y.start(source_y, land_y)
+    sends = []
+    for number, (low, high) in enumerate(plan.spans):
+        lax.fori_loop(plan.steps[number], plan.steps[number + 1], outer_product, 0)
+        pack_weight_gradient(plan, stage, wide, width, (low, high))
+        rows_of = pl.ds(low, high - low)
+        source_y = lambda i, r, rows_of=rows_of: stage.at[r, rows_of]
+        land_y = lambda i, r, rows_of=rows_of: in_y.at[i, rows_of]
+        rings_y[number].start(source_y, land_y)
+        sends.append((rings_y[number], source_y, land_y))
     build_centre(window, own, meta, slots)
-    ring_y.finish(source_y, land_y)
-    add_rows(
-        store_to(summed, 0), lambda at: stage[gy, pl.ds(at, plan.chunk)],
-        in_y, plan.ny - 1, plan.total, plan.chunk,
-    )
+    for ring, source_y, land_y in sends:
+        ring.finish(source_y, land_y)
     for part in parts:
+        add_rows(
+            store_to(summed, 0), lambda at: stage[gy, pl.ds(at, part.chunk)],
+            in_y, plan.ny - 1, part.base, part.base + part.chunk * plan.nx, part.chunk,
+        )
         part.start_first()
 
     second.finish()
@@ -686,7 +703,7 @@
         ]
         + exchange_scratch(slots, width)
         + exchange_scratch(slots, width)
-        + [pltpu.SemaphoreType.DMA((9, peers)), pltpu.SemaphoreType.DMA((9, peers))],
+        + [pltpu.SemaphoreType.DMA((11, peers)), pltpu.SemaphoreType.DMA((11, peers))],
         compiler_params=pltpu.CompilerParams(
             collective_id=0, has_side_effects=True, vmem_limit_bytes=60 * 1024 * 1024
         ),

time: 64.4 us -> 63.6 us (0.988)
  Pallas kernels: 63 us -> 62.1 us
    pallas_call x1, Pallas kernels: 59.6 us -> 58.8 us  [local(): pl.pallas_call(functools.partial(whole_kernel, sizes, plan), out_shape=(j...]
where the time goes in v5:
time: 63.6 us; the launch traced here: 63.4 us
  Pallas kernels  62.1 us (98%)
  between operations  1.29 us (2%)
    pallas_call x1, Pallas kernels, local(): pl.pallas_call(functools.partial(whole_kernel, sizes, plan), out_shape=(j...  58.8 us
    pallas_call x1, Pallas kernels, local(): pl.pallas_call(functools.partial(output_kernel, plan), out_shape=(jax.Sha...  3.34 us

profile of v5, /device:TPU:0, one launch (start us, length us, event | category | flops | bytes accessed | tf_op | source)
XLA Modules:
  0.0 63.4 jit_solution(18241332842008505414)
XLA Ops:
  1.3 58.8 %whole.1 = (bf16[2,192,512]{2,1,0:T(8,128)(2,1)}, bf16[2,192,512]{2,1,0:T(8,128)(2,1)}, bf16[4096,128]{1,0:T(8,128)(2,1)}) custom-call(s32[2,3]{1,0:T(2,128)} %fine.1, s32[2,3]{1,0:T(2,128)} %coarse_place.1, s32[2]{0:T(128)} %parents.1, s32[1]{0:T(128)S(6)} %copy.12.counts, bf16[2,192,512]{2,1,0:T(8,128)(2,1)} %skip.1, bf16[2,192,512]{2,1,0:T(8,128)(2,1)} %coarse.1, ...), custom_call_target="tpu_custom_call" | custom-call | flops 6115295232 | bytes 12582912 | tf_op jit(solution)/shard_map/whole/pallas_call | solution.py:677
  60.1 3.3 %outputs.1 = (bf16[2,192,512]{2,1,0:T(8,128)(2,1)}, bf16[2,192,512]{2,1,0:T(8,128)(2,1)}, f32[27,96,192]{2,1,0:T(8,128)}) custom-call(bf16[2,192,512]{2,1,0:T(8,128)(2,1)} %get-tuple-element.9.skip_in, bf16[2,192,512]{2,1,0:T(8,128)(2,1)} %get-tuple-element.10.coarse_in, bf16[4096,128]{1,0:T(8,128)(2,1)} %get-tuple-element.11.rows_in), custom_call_target="tpu_custom_call" | custom-call | tf_op jit(solution)/shard_map/outputs/pallas_call | solution.py:720
